TPU v7x, 256 devices: a whole 4x4x8 slice. The times are simulated.
256 devices in a mesh: dp: 32 (over x, y, core), tensor: 8 (over z).
Axes of the slice: x: 4, y: 4, z: 8, core: 2. Of those that a mesh axis runs over, the one named last changes fastest.
Arguments:
- hidden: bfloat16 [12288, 14336], P('dp', 'tensor'), may hold values from -6 to 6
- destination: int32 [12288], P('dp'), may hold values from -1 to 12287, as said below
- job_per_tile: int32 [96], P('dp'), may hold values from 0 to 7
- down_matrix: bfloat16 [14336, 4096], P('tensor', 'dp'), may hold values from -0.046875 to 0.046875
- first_adapter_factors: bfloat16 [14336, 128], P('tensor'), may hold values from -0.046875 to 0.046875
- second_adapter_factors: bfloat16 [128, 4096], replicated, may hold values from -0.09375 to 0.09375
- cotangent: bfloat16 [12288, 4096], P(('dp', 'tensor')), may hold values from -6 to 6
Outputs:
- mixed: bfloat16 [12288, 4096], P(('dp', 'tensor'))
- packed_hidden_gradient: bfloat16 [12288, 14336], P('dp', 'tensor')
- grad_a: float32 [14336, 128], P('tensor')
- second_factor_gradient: float32 [128, 4096], replicated
Inputs may be any that keep to these rules, and one draw needn't show every extreme that they name: `destination`: each loader row names the slot group * 384 + s of a data group, or -1 where no group takes it; no slot is named twice; the rows of one device name at most 12 slots of one group, and of every group some device names exactly 12; in every draw one group receives 12 rows from every device.
All inputs are finite; a program needn't handle non-finite values.
Results may differ from a plain program's by a relative error of at most 0.019.
Values may be sent and summed in bfloat16 or wider, within the bound.
No kernel may reach another device: no remote copies, remote signals or barrier semaphores. Data moves between devices by JAX's collectives and lax.ppermute only.
A program may use at most 128 MiB of HBM per device.

v0:
```python
import jax
import jax.numpy as jnp
from jax import lax
from jax.sharding import PartitionSpec as P

ADAPTER_RANK = 16


adapter_scale = 2.0


def contract_trailing(left, right):
    return lax.dot_general(
        left, right, (((1,), (1,)), ((), ())), preferred_element_type=jnp.float32
    )


def contract_leading(left, right):
    return lax.dot_general(
        left, right, (((0,), (0,)), ((), ())), preferred_element_type=jnp.float32
    )


def on_device(
    hidden,
    destination,
    job_per_tile,
    down_matrix,
    first_adapter_factors,
    second_adapter_factors,
    cotangent,
):
    group_count = lax.axis_size("dp")
    shard_count = lax.axis_size("tensor")
    group_rows = hidden.shape[0]
    hidden_unit_count = hidden.shape[1]
    capacity = group_rows // group_count
    row_live = destination >= 0
    target_group = jnp.where(row_live, destination // group_rows, group_count)
    target_slot = jnp.where(row_live, destination % group_rows, 0)
    member = (target_group[:, None] == jnp.arange(group_count, dtype=jnp.int32)[None, :]).astype(
        jnp.int32
    )
    position = jnp.sum(jnp.cumsum(member, axis=0) * member, axis=1) - 1
    send_index = jnp.where(row_live, target_group * capacity + position, group_count * capacity)
    send_rows = (
        jnp.zeros((group_count * capacity + 1, hidden_unit_count), hidden.dtype)
        .at[send_index]
        .set(hidden)
    )
    send_slots = (
        jnp.full((group_count * capacity + 1,), -1, jnp.int32).at[send_index].set(target_slot)
    )
    send_rows = send_rows[:-1].reshape(group_count, capacity, hidden_unit_count)
    send_slots = send_slots[:-1].reshape(group_count, capacity)
    got_rows, got_slots = (
        lax.all_to_all(send_rows, "dp", split_axis=0, concat_axis=0, tiled=True),
        lax.all_to_all(send_slots, "dp", split_axis=0, concat_axis=0, tiled=True),
    )
    landing = jnp.where(got_slots >= 0, got_slots, group_rows).reshape(-1).astype(jnp.int32)
    packed_hidden = (
        jnp.zeros((group_rows + 1, hidden_unit_count), hidden.dtype)
        .at[landing]
        .set(got_rows.reshape(-1, hidden_unit_count))[:group_rows]
    )
    tile_size = group_rows // job_per_tile.shape[0]
    slot_job = jnp.repeat(job_per_tile, tile_size, total_repeat_length=group_rows)
    job_of_column = jnp.arange(second_adapter_factors.shape[0], dtype=jnp.int32) // ADAPTER_RANK
    job_selector = slot_job[:, None] == job_of_column[None, :]
    inner_bits = jnp.where(
        job_selector,
        jnp.dot(packed_hidden, first_adapter_factors, preferred_element_type=jnp.float32),
        0.0,
    ).astype(jnp.bfloat16)
    complete_cotangent, inner_all = (
        lax.all_gather(cotangent, "tensor", axis=0, tiled=True),
        lax.all_gather(inner_bits, "tensor", axis=0, tiled=True),
    )
    inner_sum = jnp.sum(inner_all.reshape(shard_count, group_rows, -1).astype(jnp.float32), axis=0)
    inner_truncated = inner_sum.astype(jnp.bfloat16)
    inner_gradient = jnp.where(
        job_selector,
        adapter_scale * contract_trailing(complete_cotangent, second_adapter_factors),
        0.0,
    ).astype(jnp.bfloat16)
    full_weight = lax.all_gather(down_matrix, "dp", axis=1, tiled=True)
    base_part = jnp.dot(packed_hidden, full_weight, preferred_element_type=jnp.float32)
    backward_total = contract_trailing(complete_cotangent, full_weight)
    base_output_shard = lax.psum_scatter(
        base_part.astype(jnp.bfloat16), "tensor", scatter_dimension=0, tiled=True
    ).astype(jnp.float32)
    shard_rows = group_rows // shard_count
    inner_portion = lax.dynamic_slice_in_dim(
        inner_truncated, lax.axis_index("tensor") * shard_rows, shard_rows, 0
    )
    mixed = (
        base_output_shard
        + adapter_scale
        * jnp.dot(inner_portion, second_adapter_factors, preferred_element_type=jnp.float32)
    ).astype(jnp.bfloat16)
    packed_hidden_gradient = (
        backward_total + contract_trailing(inner_gradient, first_adapter_factors)
    ).astype(jnp.bfloat16)
    grad_a_part = contract_leading(packed_hidden, inner_gradient)
    second_factor_gradient_portion = adapter_scale * contract_leading(
        inner_truncated, complete_cotangent
    )
    grad_a, second_factor_gradient = (
        lax.psum(grad_a_part.astype(jnp.bfloat16), "dp").astype(jnp.float32),
        lax.psum(second_factor_gradient_portion.astype(jnp.bfloat16), "dp").astype(jnp.float32),
    )
    return (mixed, packed_hidden_gradient, grad_a, second_factor_gradient)


def solution(mesh):
    return jax.shard_map(
        on_device,
        mesh=mesh,
        in_specs=(
            P("dp", "tensor"),
            P("dp"),
            P("dp"),
            P("tensor", "dp"),
            P("tensor", None),
            P(),
            P(("dp", "tensor"), None),
        ),
        out_specs=(P(("dp", "tensor"), None), P("dp", "tensor"), P("tensor", None), P()),
        check_vma=False,
    )
```

profile of v0, /device:TPU:1, one launch (start us, length us, event | category | flops | bytes accessed | tf_op | source)
XLA Modules:
  0.0 316.0 jit_solution(11088751575282182553)
XLA Ops:
  7.2 0.0 copy-start
  7.2 0.0 all-gather.5.cloned.1.call-start
  7.2 0.7 all-gather.5.cloned.1.call-update
  7.9 0.0 all-gather.3.cloned.1.call-start
  8.0 0.7 all-gather.3.cloned.1.call-update
  8.7 0.7 fusion.44
  9.4 0.9 reduce-window.14
  10.3 0.2 slice_reduce_fusion
  10.5 0.7 fusion.18
  11.2 0.1 fusion.15
  11.3 0.7 fusion.19
  12.0 2.9 scatter_custom_fusion
  14.9 0.7 all_to_all.11
  15.6 8.6 %all-to-all-start = ((s32[32,1,12]{2,1,0:T(1,128)}), s32[32,1,12]{2,1,0:T(1,128)S(1)}, u32[]{:S(2)}, u32[]{:S(2)}) async-start(s32[32,1,12]{2,1,0:T(1,128)} %bitcast.2), calls=%async_computation | async-start | bytes 32768 | tf_op jit(solution)/shard_map/all_to_all | solution.py:58
  24.2 3.9 %scatter_custom_fusion.1 = bf16[385,1792]{1,0:T(8,128)(2,1)S(1)} fusion(s32[384]{0:T(512)S(1)} %get-tuple-element.19, bf16[384,1792]{1,0:T(8,128)(2,1)} %param.9, bf16[]{:T(256)} %constant.121.clone.1), kind=kCustom, calls=%fused_computation.22 | custom fusion | bytes 1380352 | tf_op jit(solution)/shard_map/scatter | solution.py:49
  28.2 1.2 slice.41
  29.3 3.3 %reshape.171 = bf16[32,12,1792]{2,1,0:T(8,128)(2,1)} reshape(bf16[384,1792]{1,0:T(8,128)(2,1)} %slice.41) | data formatting | bytes 2752512 | tf_op jit(solution)/shard_map/reshape | solution.py:54
  32.6 0.0 all-to-all-done
  32.6 7.5 %all-to-all-start.1 = ((bf16[32,12,1792]{2,1,0:T(8,128)(2,1)}), bf16[32,12,1792]{2,1,0:T(8,128)(2,1)S(1)}, u32[]{:S(2)}, u32[]{:S(2)}) async-start(bf16[32,12,1792]{2,1,0:T(8,128)(2,1)} %reshape.171), calls=%async_computation.1 | async-start | bytes 3670016 | tf_op jit(solution)/shard_map/all_to_all | solution.py:57
  40.2 0.0 all-reduce.3.cloned.1.call-start
  40.2 0.6 fusion.30
  40.8 2.0 fusion.25
  42.8 0.5 broadcast.259
  43.3 0.7 reduce.12
  44.0 0.1 all_to_all.13
  44.1 21.5 %all-to-all-done.1 = bf16[32,12,1792]{2,1,0:T(8,128)(2,1)S(1)} async-done(((bf16[32,12,1792]{2,1,0:T(8,128)(2,1)}), bf16[32,12,1792]{2,1,0:T(8,128)(2,1)S(1)}, u32[]{:S(2)}, u32[]{:S(2)}) %all-to-all-start.1) | async-done | bytes 1376288 | tf_op jit(solution)/shard_map/all_to_all | solution.py:57
  65.6 1.2 reshape.204
  66.9 3.8 %scatter_custom_fusion.2 = bf16[385,1792]{1,0:T(8,128)(2,1)S(1)} fusion(s32[384]{0:T(512)S(1)} %fusion.26, bf16[384,1792]{1,0:T(8,128)(2,1)} %reshape.204, bf16[]{:T(256)} %constant.121.clone.1), kind=kCustom, calls=%fused_computation.20 | custom fusion | bytes 1380352 | tf_op jit(solution)/shard_map/scatter | solution.py:64
  70.7 0.5 fusion.6
  71.2 24.5 %all_gather.10 = bf16[3072,128]{1,0:T(8,128)(2,1)S(1)} all-gather(bf16[384,128]{1,0:T(8,128)(2,1)S(1)} %fusion.6), channel_id=1, replica_groups=mesh['dp'=32,'tensor'=8] {'tensor'}, dimensions={0}, use_global_device_ids=true | all-gather | bytes 884736 | tf_op jit(solution)/shard_map/all_gather | solution.py:77
  95.7 0.1 reduce_sum.22
  95.8 0.0 all-gather.5.cloned.1.call-done
  95.9 3.0 fusion.5
  98.9 1.4 convolution_convert_fusion.1
  100.3 1.7 fusion
  102.0 0.0 all-reduce.3.cloned.1.call-update
  102.0 0.2 reduce-scatter.2.cloned.1.call-start
  102.3 38.5 %all-gather.3.cloned.1.call-done = bf16[1792,4096]{1,0:T(8,128)(2,1)} async-done(((bf16[1792,128]{1,0:T(8,128)(2,1)}), bf16[1792,4096]{1,0:T(8,128)(2,1)}) %all-gather.3.cloned.1.call-update) | async-done | bytes 14680080 | tf_op jit(solution)/shard_map/all_gather | solution.py:86
  140.7 12.4 %convolution_convert_fusion = bf16[384,4096]{1,0:T(8,128)(2,1)} fusion(bf16[1792,4096]{1,0:T(8,128)(2,1)} %all-gather.3.cloned.1.call-done, bf16[385,1792]{1,0:T(8,128)(2,1)S(1)} %scatter_custom_fusion.2), kind=kOutput, calls=%fused_computation.3 | convolution fusion | flops 5638717440 | bytes 19202048 | tf_op jit(solution)/shard_map/dot_general | solution.py:87
  153.1 0.0 reduce-scatter.2.cloned.1.call-update
  153.1 107.5 %all-reduce.3.cloned.1.call-done = (bf16[1792,128]{1,0:T(8,128)(2,1)}, bf16[128,4096]{1,0:T(8,128)(2,1)}) async-done(((bf16[1792,128]{1,0:T(8,128)(2,1)}, bf16[128,4096]{1,0:T(8,128)(2,1)}), (bf16[1792,128]{1,0:T(8,128)(2,1)}, bf16[128,4096]{1,0:T(8,128)(2,1)})) %all-reduce.3.cloned.1.call-update) | async-done | bytes 1507344 | tf_op jit(solution)/shard_map/psum | solution.py:109
  260.6 2.1 convert_element_type.45
  262.7 1.5 convert_element_type.47
  264.2 1.1 copy-done.2
  265.4 10.7 %fusion.31 = f32[384,1792]{1,0:T(8,128)} fusion(bf16[384,4096]{1,0:T(8,128)(2,1)S(1)} %copy-done.2, bf16[1792,4096]{1,0:T(8,128)(2,1)} %all-gather.3.cloned.1.call-done), kind=kOutput, calls=%fused_computation.64 | convolution fusion | flops 5637144576 | bytes 20578304 | tf_op jit(solution)/shard_map/dot_general | solution.py:13
  276.1 3.4 %fusion.3 = bf16[384,1792]{1,0:T(8,128)(2,1)} fusion(f32[384,1792]{1,0:T(8,128)} %fusion.31, bf16[384,128]{1,0:T(8,128)(2,1)S(1)} %fusion.5, bf16[1792,128]{1,0:T(8,128)(2,1)S(1)} %copy-done.5), kind=kOutput, calls=%fused_computation.10 | convolution fusion | flops 177537024 | bytes 4685824 | tf_op jit(solution)/shard_map/dot_general | solution.py:13
  279.5 27.9 %reduce-scatter.2.cloned.1.call-done = bf16[48,4096]{1,0:T(8,128)(2,1)} async-done(((bf16[384,4096]{1,0:T(8,128)(2,1)}), bf16[48,4096]{1,0:T(8,128)(2,1)}) %reduce-scatter.2.cloned.1.call-update) | async-done | bytes 393232 | tf_op jit(solution)/shard_map/reduce_scatter | solution.py:89
  307.4 2.0 fusion.2
  (18 shorter events, 0.1 us)
Async XLA Ops:
  7.2 88.7 %copy-start = (bf16[128,4096]{1,0:T(8,128)(2,1)S(1)}, bf16[128,4096]{1,0:T(8,128)(2,1)}, u32[]{:S(2)}) copy-start(bf16[128,4096]{1,0:T(8,128)(2,1)} %param.14) | copy-start | bytes 3145732
  7.2 88.7 %all-gather.5.cloned.1.call-start = ((), (), s32[]{:S(2)}) async-start(), calls=%async_computation.5 | async-start | bytes 3538944 | tf_op jit(solution)/shard_map/all_gather | solution.py:76
  7.9 132.8 %all-gather.3.cloned.1.call-start = ((), (), s32[]{:S(2)}) async-start(), calls=%async_computation.3 | async-start | bytes 15138816 | tf_op jit(solution)/shard_map/all_gather | solution.py:86
  15.6 16.9 %all-to-all-start = ((s32[32,1,12]{2,1,0:T(1,128)}), s32[32,1,12]{2,1,0:T(1,128)S(1)}, u32[]{:S(2)}, u32[]{:S(2)}) async-start(s32[32,1,12]{2,1,0:T(1,128)} %bitcast.2), calls=%async_computation | async-start | bytes 32768 | tf_op jit(solution)/shard_map/all_to_all | solution.py:58
  32.6 7.6 %copy-start.6 = (s32[3]{0:T(128)S(1)}, s32[3]{0:T(128)}, u32[]{:S(2)}) copy-start(s32[3]{0:T(128)} %param.11) | copy-start | bytes 40
  32.6 33.0 %all-to-all-start.1 = ((bf16[32,12,1792]{2,1,0:T(8,128)(2,1)}), bf16[32,12,1792]{2,1,0:T(8,128)(2,1)S(1)}, u32[]{:S(2)}, u32[]{:S(2)}) async-start(bf16[32,12,1792]{2,1,0:T(8,128)(2,1)} %reshape.171), calls=%async_computation.1 | async-start | bytes 3670016 | tf_op jit(solution)/shard_map/all_to_all | solution.py:57
  40.2 220.5 %all-reduce.3.cloned.1.call-start = ((), (), s32[]{:S(2)}) async-start(), calls=%async_computation.6 | async-start | bytes 3014656 | tf_op jit(solution)/shard_map/psum | solution.py:109
  66.9 3.8 %copy-start.4 = (bf16[1792,128]{1,0:T(8,128)(2,1)S(1)}, bf16[1792,128]{1,0:T(8,128)(2,1)}, u32[]{:S(2)}) copy-start(bf16[1792,128]{1,0:T(8,128)(2,1)} %param.13) | copy-start | bytes 1376260
  95.9 4.4 %copy-start.1 = (bf16[384,4096]{1,0:T(8,128)(2,1)S(1)}, bf16[384,4096]{1,0:T(8,128)(2,1)}, u32[]{:S(2)}) copy-start(bf16[384,4096]{1,0:T(8,128)(2,1)} %all-gather.5.cloned.1.call-done) | copy-start | bytes 9437188
  102.0 205.4 %reduce-scatter.2.cloned.1.call-start = ((), (), s32[]{:S(2)}) async-start(), calls=%async_computation.4 | async-start | bytes 3538944 | tf_op jit(solution)/shard_map/reduce_scatter | solution.py:89
  260.6 2.1 copy-start.3
  262.7 2.6 copy-start.2
  265.4 10.8 %copy-start.5 = (bf16[1792,128]{1,0:T(8,128)(2,1)S(1)}, bf16[1792,128]{1,0:T(8,128)(2,1)}, u32[]{:S(2)}) copy-start(bf16[1792,128]{1,0:T(8,128)(2,1)} %param.13) | copy-start | bytes 1376260
Sparse Core Ops, SparseCore 0:
  9.8 48.5 all-gather.4
  60.9 79.8 all-gather.2
  144.7 115.8 all-reduce.2
  263.2 44.1 reduce-scatter.1
where the time goes:
time: 318 us; the launch traced here: 316 us
  waiting for transfers between devices  197 us (62%)
  matrix products  35.2 us (11%)
  blocking collectives  24.5 us (8%)
  local copies, waits for them, and re-layouts  19.6 us (6%)
  starting transfers between devices  16.5 us (5%)
  between operations  13.9 us (4%)
  other arithmetic  9.53 us (3%)
    psum x1, waiting for transfers between devices, on_device(): lax.psum(grad_a_part.astype(jnp.bfloat16), 'dp').astype(jnp.float32)  107 us
    all_gather x1, waiting for transfers between devices, on_device(): full_weight = lax.all_gather(down_matrix, 'dp', axis=1, tiled=True)  38.5 us
    reduce_scatter x1, waiting for transfers between devices, on_device(): lax.psum_scatter(base_part.astype(jnp.bfloat16), 'tensor', scatter_dimens...  27.9 us
    all_gather x1, blocking collectives, on_device(): lax.all_gather(inner_bits, 'tensor', axis=0, tiled=True)  24.5 us
    all_to_all x1, waiting for transfers between devices, on_device(): lax.all_to_all(send_rows, 'dp', split_axis=0, concat_axis=0, tiled=True)  21.5 us
    dot_general x3, matrix products, contract_trailing(): lax.dot_general(left, right, (((1,), (1,)), ((), ())), preferred_element_...  17.2 us
    dot_general x1, matrix products, on_device(): jnp.dot(packed_hidden, full_weight, preferred_element_type=jnp.float32)  12.4 us
    all_to_all x1, starting transfers between devices, on_device(): lax.all_to_all(send_slots, 'dp', split_axis=0, concat_axis=0, tiled=True)  8.59 us
  transfers between devices with their start and end apart: 6, of which 4 were waited for; matrix products, arithmetic and copies ran while one was open for 19% of the time, Pallas kernels for 0%

commit v1 on v0

v1 whole, which is shorter than its diff:
```python
import functools

import jax
import jax.numpy as jnp
from jax import lax
from jax.experimental import pallas as pl
from jax.experimental.pallas import tpu as pltpu
from jax.sharding import PartitionSpec as P

ADAPTER_RANK = 16
ADAPTER_SCALE = 2.0
NX, NY, NZ = 4, 4, 8
CHIPS = NX * NY
LANES = 128
VMEM_LIMIT = 40 * 1024 * 1024
F32 = jnp.float32
BF16 = jnp.bfloat16

SAME_CORE = [[2 * chip + core for chip in range(CHIPS)] for core in range(2)]


def after(values, *others):
    return lax.optimization_barrier((values, others))[0]


def swap_core(value):
    return lax.ppermute(value, "dp", [(i, i ^ 1) for i in range(2 * CHIPS)])


def dot_nt(left, right):
    return lax.dot_general(left, right, (((1,), (1,)), ((), ())), preferred_element_type=F32)


def dot_nn(left, right):
    return jnp.dot(left, right, preferred_element_type=F32)


def dot_tn(left, right):
    return lax.dot_general(left, right, (((0,), (0,)), ((), ())), preferred_element_type=F32)


def params(limit=VMEM_LIMIT):
    return pltpu.CompilerParams(vmem_limit_bytes=limit)


VM = pl.BlockSpec(memory_space=pltpu.VMEM)
SM = pl.BlockSpec(memory_space=pltpu.SMEM)


def sort_kernel(dest_ref, hidden_ref, out_ref):
    rows, units = hidden_ref.shape
    capacity = rows // (2 * CHIPS)
    dest = dest_ref[...]
    live = dest >= 0
    dest_f = dest.astype(F32)
    group = jnp.where(live, jnp.floor((dest_f + 0.5) * (1.0 / rows)), -1.0)
    across = jnp.broadcast_to(group, (rows, rows))
    down = across.T
    sub = lax.broadcasted_iota(jnp.int32, (rows, rows), 0)
    lane = lax.broadcasted_iota(jnp.int32, (rows, rows), 1)
    earlier = jnp.where((across == down) & (sub < lane), 1.0, 0.0)
    position = jnp.sum(earlier, axis=0, keepdims=True)
    place = jnp.where(live, group * capacity + position, -1.0)
    pick = jnp.where(sub.astype(F32) == place, 1.0, 0.0).astype(BF16)
    for tile in range(units // 256):
        cols = slice(tile * 256, (tile + 1) * 256)
        out_ref[:, cols] = dot_nn(pick, hidden_ref[:, cols]).astype(BF16)
    chip = jnp.floor((dest_f + 0.5) * (1.0 / (2 * rows)))
    code = jnp.where(live, dest_f - chip * (2 * rows) + 1.0, 0.0)
    high = jnp.floor(code * (1.0 / 16.0))
    low = code - 16.0 * high
    row = lax.broadcasted_iota(jnp.int32, (LANES, rows), 0)
    codes = jnp.where(row == 0, high, jnp.where(row == 1, low, 0.0)).astype(BF16)
    out_ref[:, units:] = dot_nt(pick, codes).astype(BF16)


def sort_rows(destination, hidden):
    rows, units = hidden.shape
    return pl.pallas_call(
        sort_kernel,
        out_shape=jax.ShapeDtypeStruct((rows, units + LANES), BF16),
        in_specs=[VM, VM],
        out_specs=VM,
        compiler_params=params(),
    )(destination.reshape(1, rows), hidden)


def pack_kernel(core_ref, mine_ref, other_ref, out_ref):
    slots, units = out_ref.shape
    rows = mine_ref.shape[0]
    weight_row = lax.broadcasted_iota(jnp.int32, (8, LANES), 1)
    weight = jnp.where(weight_row == 0, 16.0, jnp.where(weight_row == 1, 1.0, 0.0)).astype(BF16)
    wanted = lax.broadcasted_iota(jnp.int32, (slots, rows), 0) + core_ref[0] * slots + 1
    wanted = wanted.astype(F32)
    picks = []
    for got in (mine_ref, other_ref):
        code = dot_nt(weight, got[:, units:])[0:1, :]
        picks.append(jnp.where(wanted == code, 1.0, 0.0).astype(BF16))
    for tile in range(units // 256):
        cols = slice(tile * 256, (tile + 1) * 256)
        out_ref[:, cols] = (
            dot_nn(picks[0], mine_ref[:, cols]) + dot_nn(picks[1], other_ref[:, cols])
        ).astype(BF16)


def pack_rows(core, mine, other):
    rows, wide = mine.shape
    return pl.pallas_call(
        pack_kernel,
        out_shape=jax.ShapeDtypeStruct((rows, wide - LANES), BF16),
        in_specs=[SM, VM, VM],
        out_specs=VM,
        compiler_params=params(),
    )(core.reshape(1), mine, other)


def cotangent_kernel(z_ref, jobs_ref, cot_ref, second_ref, out_ref):
    rows, model = cot_ref.shape
    inner = ADAPTER_SCALE * dot_nt(cot_ref[...], second_ref[...])
    width = inner.shape[1]
    slot = lax.broadcasted_iota(jnp.int32, (rows, width), 0) + z_ref[0] * rows
    tile = NZ * rows // 3
    job = jnp.where(slot < tile, jobs_ref[0], jnp.where(slot < 2 * tile, jobs_ref[1], jobs_ref[2]))
    column = lax.broadcasted_iota(jnp.int32, (rows, width), 1)
    first = job * ADAPTER_RANK
    chosen = (column >= first) & (column < first + ADAPTER_RANK)
    out_ref[:, :model] = cot_ref[...]
    out_ref[:, model:] = jnp.where(chosen, inner, 0.0).astype(BF16)


def widen_cotangent(z, jobs, cotangent, second):
    rows, model = cotangent.shape
    return pl.pallas_call(
        cotangent_kernel,
        out_shape=jax.ShapeDtypeStruct((rows, model + second.shape[0]), BF16),
        in_specs=[SM, SM, VM, VM],
        out_specs=VM,
        compiler_params=params(),
    )(z.reshape(1), jobs, cotangent, second)


def order_kernel(half, z_ref, *refs):
    pieces, (model_ref, inner_ref, sem) = refs[:-3], refs[-3:]
    model = model_ref.shape[2]
    copies = []

    def copy(source, out_ref, offset, start, size):
        spot = lax.rem(z_ref[0] + (offset + NZ), NZ)
        copies.append(
            pltpu.make_async_copy(
                source, out_ref.at[spot, :, pl.ds(start, size)], sem.at[len(copies)]
            )
        )
        copies[-1].start()

    for piece, offset in zip(pieces[:-2], range(1 - NZ // 2, NZ // 2)):
        copy(piece.at[:, pl.ds(0, model)], model_ref, offset, 0, model)
        copy(piece.at[:, pl.ds(model, LANES)], inner_ref, offset, 0, LANES)
    low, high = pieces[-2:]
    copy(low, model_ref, NZ // 2, 0, half)
    copy(high.at[:, pl.ds(0, model - half)], model_ref, NZ // 2, half, model - half)
    copy(high.at[:, pl.ds(model - half, LANES)], inner_ref, NZ // 2, 0, LANES)
    for started in copies:
        started.wait()


def send_z(value, step):
    return lax.ppermute(value, "tensor", [(i, (i + step) % NZ) for i in range(NZ)])


def gather_z(piece, z):
    rows, wide = piece.shape
    half = wide // (2 * LANES) * LANES
    up = down = piece
    pieces = [piece]
    for step in range(1, NZ // 2):
        up, down = lax.optimization_barrier((send_z(up, 1), send_z(down, -1)))
        pieces = [up] + pieces + [down]
        if step == 2:
            between = (up, down)
    pieces += lax.optimization_barrier((send_z(up[:, :half], 1), send_z(down[:, half:], -1)))
    anywhere = pl.BlockSpec(memory_space=pl.ANY)
    model, inner = pl.pallas_call(
        functools.partial(order_kernel, half),
        out_shape=(
            jax.ShapeDtypeStruct((NZ, rows, wide - LANES), BF16),
            jax.ShapeDtypeStruct((NZ, rows, LANES), BF16),
        ),
        in_specs=[SM] + [anywhere] * len(pieces),
        out_specs=(VM, VM),
        scratch_shapes=[pltpu.SemaphoreType.DMA((2 * NZ + 1,))],
        compiler_params=params(),
    )(z.reshape(1), *pieces)
    return model.reshape(NZ * rows, -1), inner.reshape(NZ * rows, LANES), between


def sum_z(value):
    step = 1
    while step < NZ:
        value = value + lax.ppermute(value, "tensor", [(i, i ^ step) for i in range(NZ)])
        step *= 2
    return value


def gather_xor(value):
    step = 1
    while step < NZ:
        other = lax.ppermute(value, "tensor", [(i, i ^ step) for i in range(NZ)])
        value = jnp.concatenate([value, other], axis=0)
        step *= 2
    return value


def share_kernel(z_ref, inner_ref, cot_ref, first_ref, out_ref):
    parts, rows, _ = out_ref.shape
    firsts = first_ref.shape[0] // parts
    seconds = rows - firsts
    wide = cot_ref.shape[1] // NZ
    column = pl.multiple_of(z_ref[0] * wide, LANES)
    block = ADAPTER_SCALE * dot_nn(inner_ref[...], cot_ref[:, pl.ds(column, wide)])
    block = block.astype(BF16)
    each = block.shape[0] // seconds
    for i in range(parts):
        out_ref[i, :firsts, :] = first_ref[i * firsts : (i + 1) * firsts, :]
        row, column = (i % each) * seconds, (i // each) * LANES
        out_ref[i, firsts:, :] = block[row : row + seconds, column : column + LANES]


def shares(z, inner, cotangent, first_part):
    parts = 2 * CHIPS
    rows = first_part.shape[0] // parts + inner.shape[0] * cotangent.shape[1] // (NZ * parts * LANES)
    return pl.pallas_call(
        share_kernel,
        out_shape=jax.ShapeDtypeStruct((parts, rows, LANES), BF16),
        in_specs=[SM, VM, VM, VM],
        out_specs=VM,
        compiler_params=params(),
    )(z.reshape(1), inner, cotangent, first_part)


def finish_kernel(z_ref, every_ref, first_ref, second_ref):
    parts, rows, _ = every_ref.shape
    firsts = first_ref.shape[0] // parts
    seconds = (rows - firsts) // NZ
    each = second_ref.shape[0] // seconds
    wide = second_ref.shape[1] // NZ
    for i in range(parts):
        first_ref[i * firsts : (i + 1) * firsts, :] = every_ref[i, :firsts, :].astype(F32)
        share = every_ref[i, firsts:, :].astype(F32)
        row = (i % each) * seconds
        for place in range(NZ):
            column = (z_ref[0] ^ place) * wide + (i // each) * LANES
            second_ref[row : row + seconds, pl.ds(pl.multiple_of(column, LANES), LANES)] = share[
                place * seconds : (place + 1) * seconds
            ]


def finish(z, every, units, width, model):
    return pl.pallas_call(
        finish_kernel,
        out_shape=(
            jax.ShapeDtypeStruct((units, width), F32),
            jax.ShapeDtypeStruct((width, model), F32),
        ),
        in_specs=[SM, VM],
        out_specs=(VM, VM),
        compiler_params=params(),
    )(z.reshape(1), every)


def forward_kernel(packed_ref, weight_ref, out_ref):
    out_ref[...] = dot_nt(packed_ref[...], weight_ref[...]).astype(BF16)


def forward(packed, weight):
    (slots, units), model = packed.shape, weight.shape[0]
    tile = 1024
    return pl.pallas_call(
        forward_kernel,
        grid=(model // tile,),
        out_shape=jax.ShapeDtypeStruct((slots, model), BF16),
        in_specs=[
            pl.BlockSpec((slots, units), lambda i: (0, 0)),
            pl.BlockSpec((tile, units), lambda i: (i, 0)),
        ],
        out_specs=pl.BlockSpec((slots, tile), lambda i: (0, i)),
        compiler_params=params(),
        cost_estimate=pl.CostEstimate(
            flops=2 * slots * units * model,
            bytes_accessed=2 * (slots * units + units * model + slots * model),
            transcendentals=0,
        ),
    )(packed, weight)


def backward_kernel(cot_ref, inner_ref, weight_ref, first_ref, out_ref):
    total = dot_nn(cot_ref[...], weight_ref[...]) + dot_nt(inner_ref[...], first_ref[...])
    out_ref[...] = total.astype(BF16)


def backward(cotangent, inner_gradient, weight, first_factors):
    (slots, model), units = cotangent.shape, weight.shape[1]
    tile = 896
    return pl.pallas_call(
        backward_kernel,
        grid=(units // tile,),
        out_shape=jax.ShapeDtypeStruct((slots, units), BF16),
        in_specs=[
            pl.BlockSpec((slots, model), lambda i: (0, 0)),
            pl.BlockSpec((slots, LANES), lambda i: (0, 0)),
            pl.BlockSpec((model, tile), lambda i: (0, i)),
            pl.BlockSpec((tile, LANES), lambda i: (i, 0)),
        ],
        out_specs=pl.BlockSpec((slots, tile), lambda i: (0, i)),
        compiler_params=params(),
        cost_estimate=pl.CostEstimate(
            flops=2 * slots * units * model,
            bytes_accessed=2 * (slots * units + units * model + slots * model),
            transcendentals=0,
        ),
    )(cotangent, inner_gradient, weight, first_factors)


def on_device(hidden, destination, job_per_tile, down_matrix, first_factors, second_factors, cotangent):
    rows, units = hidden.shape
    shard = rows // NZ
    width, model = second_factors.shape
    core = lax.rem(lax.axis_index("dp"), 2)
    z = lax.axis_index("tensor")

    weight = lax.all_gather(down_matrix.T, "dp", axis=0, tiled=True)
    sent = sort_rows(destination, hidden)
    got = lax.all_to_all(
        sent, "dp", split_axis=0, concat_axis=0, axis_index_groups=SAME_CORE, tiled=True
    )
    piece = widen_cotangent(z, job_per_tile, cotangent, second_factors)
    full_cotangent, inner_gradient, between = gather_z(piece, z)
    got = after(got, *between)

    packed = pack_rows(core, got, swap_core(got))
    slot_job = jnp.repeat(job_per_tile, rows // job_per_tile.shape[0], total_repeat_length=rows)
    column = jnp.arange(width, dtype=jnp.int32)
    column_job = column // ADAPTER_RANK
    inner_part = jnp.where(
        slot_job[:, None] == column_job[None, :], dot_nn(packed, first_factors), 0.0
    ).astype(BF16)
    fold = (column[None, :] % ADAPTER_RANK == jnp.arange(ADAPTER_RANK)[:, None]).astype(BF16)
    inner_sum = sum_z(dot_nt(fold, inner_part)).astype(BF16)
    inner = jnp.where(
        slot_job[None, :] == column_job[:, None], jnp.tile(inner_sum, (width // ADAPTER_RANK, 1)), 0
    ).astype(BF16)
    my_slots = (
        jnp.arange(rows, dtype=jnp.int32)[:, None]
        == z * shard + jnp.arange(shard, dtype=jnp.int32)[None, :]
    ).astype(BF16)
    my_inner = lax.dot_general(
        my_slots, inner, (((0,), (1,)), ((), ())), preferred_element_type=F32
    ).astype(BF16)

    first_part = dot_tn(packed, inner_gradient).astype(BF16)
    sums = shares(z, inner, full_cotangent, first_part)
    parts = lax.all_to_all(sums, "dp", split_axis=0, concat_axis=0, tiled=True)
    share = jnp.sum(parts.astype(F32), axis=0).astype(BF16)
    firsts = units // (2 * CHIPS)
    share = jnp.concatenate([share[:firsts], gather_xor(share[firsts:])], axis=0)
    spread = jnp.broadcast_to(share[None], (2 * CHIPS,) + share.shape)
    every = lax.all_to_all(spread, "dp", split_axis=0, concat_axis=0, tiled=True)

    weight = after(weight, sums)
    base = after(forward(packed, weight), parts)
    summed = lax.psum_scatter(base, "tensor", scatter_dimension=0, tiled=True)
    hidden_gradient = backward(full_cotangent, inner_gradient, weight, first_factors)
    grad_a, second_gradient = finish(z, after(every, hidden_gradient), units, width, model)
    mixed = (
        summed.astype(F32) + ADAPTER_SCALE * dot_nn(my_inner, second_factors)
    ).astype(BF16)
    return (mixed, hidden_gradient, grad_a, second_gradient)


def solution(mesh):
    return jax.shard_map(
        on_device,
        mesh=mesh,
        in_specs=(
            P("dp", "tensor"),
            P("dp"),
            P("dp"),
            P("tensor", "dp"),
            P("tensor", None),
            P(),
            P(("dp", "tensor"), None),
        ),
        out_specs=(P(("dp", "tensor"), None), P("dp", "tensor"), P("tensor", None), P()),
        check_vma=False,
    )
```

time: 318 us -> 172 us (0.54)
  waiting for transfers between devices: 197 us -> 46.5 us
  starting transfers between devices: 16.5 us -> 55.4 us
  Pallas kernels: 0 us -> 31.3 us
  matrix products: 35.2 us -> 4.77 us
  blocking collectives: 24.5 us -> 0 us
  other arithmetic: 9.53 us -> 2.23 us
    psum x1 -> x0, waiting for transfers between devices: 107 us -> none  [on_device(): lax.psum(grad_a_part.astype(jnp.bfloat16), 'dp').astype(jnp.float32)]
    all_gather x2 -> x1, waiting for transfers between devices: 38.5 us -> 0.02 us  [on_device(): weight = lax.all_gather(down_matrix.T, 'dp', axis=0, tiled=True)]
    ppermute x0 -> x15, waiting for transfers between devices: none -> 36.4 us  [the longest x8 23.9 us: send_z(): lax.ppermute(value, 'tensor', [(i, (i + step) % NZ) for i in range(NZ)])]
    pallas_call x0 -> x8, Pallas kernels: none -> 31.3 us  [the longest x1 11.3 us: backward(): pl.pallas_call(backward_kernel, grid=(units // tile,), out_shape=jax.Shap...]
    dot_general x8 -> x3, matrix products: 35.2 us -> 4.77 us  [the longest x1 2.25 us: dot_nn(): return jnp.dot(left, right, preferred_element_type=F32)]
    ppermute x0 -> x15, starting transfers between devices: none -> 28.1 us  [the longest x8 15.3 us: send_z(): lax.ppermute(value, 'tensor', [(i, (i + step) % NZ) for i in range(NZ)])]
    reduce_scatter x1, waiting for transfers between devices: 27.9 us -> 0.01 us  [on_device(): summed = lax.psum_scatter(base, 'tensor', scatter_dimension=0, tiled=True)]
    all_gather x1 -> x0, blocking collectives: 24.5 us -> none  [on_device(): lax.all_gather(inner_bits, 'tensor', axis=0, tiled=True)]
  transfers between devices with their start and end apart: 6 -> 20, of which waited for: 4 -> 11; matrix products, arithmetic and copies ran while one was open for 19% -> 5% of each run, Pallas kernels for 0% -> 18%
where the time goes in v1:
time: 172 us; the launch traced here: 171 us
  starting transfers between devices  55.4 us (32%)
  waiting for transfers between devices  46.5 us (27%)
  Pallas kernels  31.3 us (18%)
  local copies, waits for them, and re-layouts  16.8 us (10%)
  between operations  14.4 us (8%)
  matrix products  4.77 us (3%)
  other arithmetic  2.23 us (1%)
    ppermute x8, waiting for transfers between devices, send_z(): lax.ppermute(value, 'tensor', [(i, (i + step) % NZ) for i in range(NZ)])  23.9 us
    ppermute x8, starting transfers between devices, send_z(): lax.ppermute(value, 'tensor', [(i, (i + step) % NZ) for i in range(NZ)])  15.3 us
    unnamed x45, local copies, waits for them, and re-layouts  13.4 us
    pallas_call x1, Pallas kernels, backward(): pl.pallas_call(backward_kernel, grid=(units // tile,), out_shape=jax.Shap...  11.3 us
    all_to_all x1, starting transfers between devices, on_device(): parts = lax.all_to_all(sums, 'dp', split_axis=0, concat_axis=0, tiled=True)  9.76 us
    all_to_all x1, starting transfers between devices, on_device(): lax.all_to_all(spread, 'dp', split_axis=0, concat_axis=0, tiled=True)  9.75 us
    pallas_call x1, Pallas kernels, forward(): pl.pallas_call(forward_kernel, grid=(model // tile,), out_shape=jax.Shape...  9.18 us
    all_to_all x1, waiting for transfers between devices, on_device(): lax.all_to_all(spread, 'dp', split_axis=0, concat_axis=0, tiled=True)  8.68 us
  transfers between devices with their start and end apart: 20, of which 11 were waited for; matrix products, arithmetic and copies ran while one was open for 5% of the time, Pallas kernels for 18%

profile of v1, /device:TPU:1, one launch (start us, length us, event | category | flops | bytes accessed | tf_op | source)
XLA Modules:
  0.0 171.4 jit_solution(9281434297777737039)
XLA Ops:
  7.2 2.1 %copy.11 = bf16[1792,128]{0,1:T(8,128)(2,1)} copy(bf16[1792,128]{1,0:T(8,128)(2,1)} %param.12) | data formatting | bytes 917504 | tf_op args[3]
  9.4 2.2 %shard_map.102 = bf16[384,1920]{1,0:T(8,128)(2,1)} custom-call(s32[1,384]{1,0:T(1,128)S(1)} %reshape.186.dest_ref, bf16[384,1792]{1,0:T(8,128)(2,1)S(1)} %copy-done.5), custom_call_target="tpu_custom_call" | custom-call | tf_op jit(solution)/shard_map/pallas_call | solution.py:79
  11.6 7.7 %all-to-all-start = ((bf16[16,24,1920]{2,1,0:T(8,128)(2,1)}), bf16[16,24,1920]{2,1,0:T(8,128)(2,1)S(1)}, u32[]{:S(2)}, u32[]{:S(2)}) async-start(bf16[16,24,1920]{2,1,0:T(8,128)(2,1)} %bitcast.1), calls=%async_computation | async-start | bytes 2949120 | tf_op jit(solution)/shard_map/all_to_all | solution.py:333
  19.4 1.0 copy-done.16
  20.4 1.0 shard_map.103.refs_3_
  21.4 5.7 %collective-permute-start.1 = (bf16[48,4224]{1,0:T(8,128)(2,1)S(1)}, bf16[48,4224]{1,0:T(8,128)(2,1)S(1)}, u32[]{:S(2)}, u32[]{:S(2)}) collective-permute-start(bf16[48,4224]{1,0:T(8,128)(2,1)S(1)} %shard_map.103.refs_3_), channel_id=1, source_target_pairs={{0,7},{1,0},{2,1},{3,2},{4,3},{5,4},{6,5},{7,6},{8,15},{9,8},{10,9... | collective-permute-start | bytes 1216520 | tf_op jit(solution)/shard_map/ppermute | solution.py:168
  27.0 7.7 %collective-permute-done.1.refs_4_ = bf16[48,4224]{1,0:T(8,128)(2,1)S(1)} collective-permute-done((bf16[48,4224]{1,0:T(8,128)(2,1)S(1)}, bf16[48,4224]{1,0:T(8,128)(2,1)S(1)}, u32[]{:S(2)}, u32[]{:S(2)}) %collective-permute-start.1) | collective-permute-done | bytes 405536 | tf_op jit(solution)/shard_map/ppermute | solution.py:168
  34.8 3.2 %collective-permute-done.refs_2_ = bf16[48,4224]{1,0:T(8,128)(2,1)S(1)} collective-permute-done((bf16[48,4224]{1,0:T(8,128)(2,1)S(1)}, bf16[48,4224]{1,0:T(8,128)(2,1)S(1)}, u32[]{:S(2)}, u32[]{:S(2)}) %collective-permute-start) | collective-permute-done | bytes 405536 | tf_op jit(solution)/shard_map/ppermute | solution.py:168
  38.0 0.7 copy-done.12
  38.7 2.7 %collective-permute-start.3 = (bf16[48,4224]{1,0:T(8,128)(2,1)S(1)}, bf16[48,4224]{1,0:T(8,128)(2,1)}, u32[]{:S(2)}, u32[]{:S(2)}) collective-permute-start(bf16[48,4224]{1,0:T(8,128)(2,1)S(1)} %collective-permute-done.1.refs_4_), channel_id=1, source_target_pairs={{0,7},{1,0},{2,1},{3,2},{4,3},{5,4},{6,5},{7,6},{8,15},{9,8},{10,9... | collective-permute-start | bytes 1216520 | tf_op jit(solution)/shard_map/ppermute | solution.py:168
  41.4 0.8 copy-done.10
  42.2 5.8 %collective-permute-done.2.refs_1_ = bf16[48,4224]{1,0:T(8,128)(2,1)S(1)} collective-permute-done((bf16[48,4224]{1,0:T(8,128)(2,1)S(1)}, bf16[48,4224]{1,0:T(8,128)(2,1)S(1)}, u32[]{:S(2)}, u32[]{:S(2)}) %collective-permute-start.2) | collective-permute-done | bytes 405536 | tf_op jit(solution)/shard_map/ppermute | solution.py:168
  48.0 3.0 %collective-permute-start.4 = (bf16[384,1920]{1,0:T(8,128)(2,1)S(1)}, bf16[384,1920]{1,0:T(8,128)(2,1)}, u32[]{:S(2)}, u32[]{:S(2)}) collective-permute-start(bf16[384,1920]{1,0:T(8,128)(2,1)S(1)} %bitcast.38), channel_id=1, source_target_pairs={{0,8},{8,0},{16,24},{24,16},{32,40},{40,32},{48,56},{56,48},{64,72... | collective-permute-start | bytes 4423688 | tf_op jit(solution)/shard_map/ppermute | solution.py:27
  51.7 0.7 copy-done.14
  52.4 3.5 %collective-permute-start.9 = (bf16[48,4224]{1,0:T(8,128)(2,1)}, bf16[48,4224]{1,0:T(8,128)(2,1)S(1)}, u32[]{:S(2)}, u32[]{:S(2)}) collective-permute-start(bf16[48,4224]{1,0:T(8,128)(2,1)} %collective-permute-done.3.refs_5_), channel_id=1, source_target_pairs={{0,7},{1,0},{2,1},{3,2},{4,3},{5,4},{6,5},{7,6},{8,15},{9,8},{10,9... | collective-permute-start | bytes 1216520 | tf_op jit(solution)/shard_map/ppermute | solution.py:168
  55.9 2.0 %fusion.18 = s32[384]{0:T(512)S(1)} fusion(s32[1,1,3,128]{3,2,1,0:T(4,128)S(1)} %get-tuple-element.52, s32[1,1,3,128]{3,2,1,0:T(4,128)S(1)} %get-tuple-element.51, s32[]{:T(128)} %bitcast.7, s32[]{:T(128)} %bitcast.9, s32[]{:T(128)} %bitcast.8), kind=kLoop, calls=%fused_computation.34 | loop fusion | flops 2304 | bytes 4620 | tf_op jit(solution)/shard_map/jit(_take)/gather | solution.py:341
  57.9 7.1 %collective-permute-done.8.refs_0_ = bf16[48,4224]{1,0:T(8,128)(2,1)S(1)} collective-permute-done((bf16[48,4224]{1,0:T(8,128)(2,1)S(1)}, bf16[48,4224]{1,0:T(8,128)(2,1)S(1)}, u32[]{:S(2)}, u32[]{:S(2)}) %collective-permute-start.8) | collective-permute-done | bytes 405536 | tf_op jit(solution)/shard_map/ppermute | solution.py:168
  65.1 0.8 slice.27
  65.8 0.7 copy-done.8
  67.2 0.7 slice.28
  67.9 2.8 %collective-permute-start.11 = (bf16[48,2176]{1,0:T(8,128)(2,1)}, bf16[48,2176]{1,0:T(8,128)(2,1)S(1)}, u32[]{:S(2)}, u32[]{:S(2)}) collective-permute-start(bf16[48,2176]{1,0:T(8,128)(2,1)} %slice.28), channel_id=1, source_target_pairs={{0,7},{1,0},{2,1},{3,2},{4,3},{5,4},{6,5},{7,6},{8,15},{9,8},{10,9... | collective-permute-start | bytes 626696 | tf_op jit(solution)/shard_map/ppermute | solution.py:168
  70.7 3.1 %shard_map.104.packed_ref = bf16[384,1792]{1,0:T(8,128)(2,1)S(1)} custom-call(s32[1]{0:T(128)} %bitcast.core_ref, bf16[384,1920]{1,0:T(8,128)(2,1)S(1)} %bitcast.39, bf16[384,1920]{1,0:T(8,128)(2,1)} %collective-permute-done.4.other_ref), custom_call_target="tpu_custom_call" | custom-call | tf_op jit(solution)/shard_map/pallas_call | solution.py:108
  73.9 1.9 %fusion.3 = f32[16,384]{1,0:T(8,128)S(1)} fusion(bf16[384,1792]{1,0:T(8,128)(2,1)S(1)} %shard_map.104.packed_ref, bf16[1792,128]{1,0:T(8,128)(2,1)} %first_ref.1, s32[128]{0:T(128)S(1)} %get-tuple-element.54, s32[384]{0:T(512)S(1)} %and_select_fusion.2, s32[128]{0:T(128)S(1)} %get-tuple-element.53), kind=kOutput, calls=%fused_computation.6 | convolution fusion | flops 177883136 | bytes 1862144 | tf_op jit(solution)/shard_map/dot_general | solution.py:31
  75.8 3.1 %collective-permute-done.5 = f32[16,384]{1,0:T(8,128)S(1)} collective-permute-done((f32[16,384]{1,0:T(8,128)S(1)}, f32[16,384]{1,0:T(8,128)S(1)}, u32[]{:S(2)}, u32[]{:S(2)}) %collective-permute-start.5) | collective-permute-done | bytes 24608 | tf_op jit(solution)/shard_map/ppermute | solution.py:200
  79.4 1.0 copy-done.13
  80.4 1.0 copy-done.15
  81.4 1.5 shard_map.105
  82.9 3.1 %collective-permute-start.7 = (f32[16,384]{1,0:T(8,128)S(1)}, f32[16,384]{1,0:T(8,128)S(1)}, u32[]{:S(2)}, u32[]{:S(2)}) collective-permute-start(f32[16,384]{1,0:T(8,128)S(1)} %add.114), channel_id=1, source_target_pairs={{0,4},{1,5},{2,6},{3,7},{4,0},{5,1},{6,2},{7,3},{8,12},{9,13},{10,... | collective-permute-start | bytes 73736 | tf_op jit(solution)/shard_map/ppermute | solution.py:200
  86.6 3.3 %collective-permute-done.7 = f32[16,384]{1,0:T(8,128)S(1)} collective-permute-done((f32[16,384]{1,0:T(8,128)S(1)}, f32[16,384]{1,0:T(8,128)S(1)}, u32[]{:S(2)}, u32[]{:S(2)}) %collective-permute-start.7) | collective-permute-done | bytes 24608 | tf_op jit(solution)/shard_map/ppermute | solution.py:200
  90.0 1.1 shard_map.106
  91.1 1.6 copy-done.2
  92.7 9.8 %all-to-all-start.1 = ((bf16[32,72,128]{2,1,0:T(8,128)(2,1)}), bf16[32,72,128]{2,1,0:T(8,128)(2,1)S(1)}, u32[]{:S(2)}, u32[]{:S(2)}) async-start(bf16[32,72,128]{2,1,0:T(8,128)(2,1)} %shard_map.106), calls=%async_computation.1 | async-start | bytes 1179648 | tf_op jit(solution)/shard_map/all_to_all | solution.py:362
  102.6 9.2 %shard_map.107 = bf16[384,4096]{1,0:T(8,128)(2,1)S(1)} custom-call(bf16[384,1792]{1,0:T(8,128)(2,1)S(1)} %shard_map.104.packed_ref, bf16[4096,1792]{1,0:T(8,128)(2,1)} %all-gather.2.cloned.1.call-done.weight_ref), custom_call_target="tpu_custom_call" | custom-call | flops 5637144576 | bytes 19202048 | tf_op jit(solution)/shard_map/pallas_call | solution.py:278
  111.8 1.6 copy-done.4
  113.4 1.4 all-to-all-done.1
  114.9 1.0 collective-permute-start.12
  115.9 1.5 collective-permute-done.12
  117.5 2.2 %collective-permute-start.13 = (bf16[32,128]{1,0:T(8,128)(2,1)S(1)}, bf16[32,128]{1,0:T(8,128)(2,1)S(1)}, u32[]{:S(2)}, u32[]{:S(2)}) collective-permute-start(bf16[32,128]{1,0:T(8,128)(2,1)S(1)} %pad_maximum_fusion.2), channel_id=1, source_target_pairs={{0,2},{1,3},{2,0},{3,1},{4,6},{5,7},{6,4},{7,5},{8,10},{9,11},{10,... | collective-permute-start | bytes 24584 | tf_op jit(solution)/shard_map/ppermute | solution.py:208
  119.6 1.2 collective-permute-done.13
  120.9 3.2 %collective-permute-start.14 = (bf16[64,128]{1,0:T(8,128)(2,1)S(1)}, bf16[64,128]{1,0:T(8,128)(2,1)S(1)}, u32[]{:S(2)}, u32[]{:S(2)}) collective-permute-start(bf16[64,128]{1,0:T(8,128)(2,1)S(1)} %pad_maximum_fusion.1), channel_id=1, source_target_pairs={{0,4},{1,5},{2,6},{3,7},{4,0},{5,1},{6,2},{7,3},{8,12},{9,13},{10,... | collective-permute-start | bytes 49160 | tf_op jit(solution)/shard_map/ppermute | solution.py:208
  124.0 3.3 %collective-permute-done.14 = bf16[64,128]{1,0:T(8,128)(2,1)S(1)} collective-permute-done((bf16[64,128]{1,0:T(8,128)(2,1)S(1)}, bf16[64,128]{1,0:T(8,128)(2,1)S(1)}, u32[]{:S(2)}, u32[]{:S(2)}) %collective-permute-start.14) | collective-permute-done | bytes 16416 | tf_op jit(solution)/shard_map/ppermute | solution.py:208
  127.4 1.3 broadcast_in_dim.39
  128.7 9.7 %all-to-all-start.2 = ((bf16[32,184,128]{2,1,0:T(8,128)(2,1)}), bf16[32,184,128]{2,1,0:T(8,128)(2,1)S(1)}, u32[]{:S(2)}, u32[]{:S(2)}) async-start(bf16[32,184,128]{2,1,0:T(8,128)(2,1)} %broadcast_in_dim.39), calls=%async_computation.3 | async-start | bytes 3014656 | tf_op jit(solution)/shard_map/all_to_all | solution.py:367
  138.5 1.9 %copy-done.3 = bf16[8,48,4096]{2,1,0:T(8,128)(2,1)S(1)} copy-done((bf16[8,48,4096]{2,1,0:T(8,128)(2,1)S(1)}, bf16[8,48,4096]{2,1,0:T(8,128)(2,1)}, u32[]{:S(2)}) %copy-start.3) | copy-done | bytes 3145752
  140.4 11.3 %shard_map.108 = bf16[384,1792]{1,0:T(8,128)(2,1)} custom-call(bf16[384,4096]{1,0:T(8,128)(2,1)S(1)} %bitcast.41, bf16[384,128]{1,0:T(8,128)(2,1)S(1)} %bitcast.43, bf16[4096,1792]{1,0:T(8,128)(2,1)} %all-gather.2.cloned.1.call-done.weight_ref, bf16[1792,128]{1,0:T(8,128)(2,1)S(1)} %copy-done.20), custom_call_target="tpu_custom_call" | custom-call | flops 5637144576 | bytes 19202048 | tf_op jit(solution)/shard_map/pallas_call | solution.py:304
  151.7 8.7 %all-to-all-done.2.every_ref = bf16[32,184,128]{2,1,0:T(8,128)(2,1)S(1)} async-done(((bf16[32,184,128]{2,1,0:T(8,128)(2,1)}), bf16[32,184,128]{2,1,0:T(8,128)(2,1)S(1)}, u32[]{:S(2)}, u32[]{:S(2)}) %all-to-all-start.2) | async-done | bytes 1507360 | tf_op jit(solution)/shard_map/all_to_all | solution.py:367
  160.4 1.9 %shard_map.109 = (f32[1792,128]{1,0:T(8,128)}, f32[128,4096]{1,0:T(8,128)}) custom-call(s32[1]{0:T(128)} %bitcast.3.z_ref, bf16[32,184,128]{2,1,0:T(8,128)(2,1)S(1)} %all-to-all-done.2.every_ref), custom_call_target="tpu_custom_call" | custom-call | tf_op jit(solution)/shard_map/pallas_call | solution.py:259
  162.3 2.3 %fusion.1 = bf16[48,4096]{1,0:T(8,128)(2,1)} fusion(bf16[128,4096]{1,0:T(8,128)(2,1)S(1)} %copy-done.1, bf16[128,384]{1,0:T(8,128)(2,1)S(1)} %compare_select_fusion.inner_ref, bf16[48,4096]{1,0:T(8,128)(2,1)} %reduce-scatter.2.cloned.1.call-done, s32[48]{0:T(128)S(1)} %iota_add_fusion.1), kind=kOutput, calls=%fused_computation.2 | convolution fusion | flops 55879680 | bytes 1933504 | tf_op jit(solution)/shard_map/dot_general | solution.py:35
  (69 shorter events, 2.8 us)
Async XLA Ops:
  7.2 2.2 %copy-start.21 = (s32[384]{0:T(512)S(1)}, s32[384]{0:T(512)}, u32[]{:S(2)}) copy-start(s32[384]{0:T(512)} %param.10) | copy-start | bytes 4612
  7.2 2.2 %copy-start.5 = (bf16[384,1792]{1,0:T(8,128)(2,1)S(1)}, bf16[384,1792]{1,0:T(8,128)(2,1)}, u32[]{:S(2)}) copy-start(bf16[384,1792]{1,0:T(8,128)(2,1)} %hidden_ref.1) | copy-start | bytes 4128772
  7.2 95.4 %all-gather.2.cloned.1.call-start = ((), (), s32[]{:S(2)}) async-start(), calls=%async_computation.4 | async-start | bytes 15138816 | tf_op jit(solution)/shard_map/all_gather | solution.py:331
  11.6 7.7 %copy-start = (bf16[128,4096]{1,0:T(8,128)(2,1)S(1)}, bf16[128,4096]{1,0:T(8,128)(2,1)}, u32[]{:S(2)}) copy-start(bf16[128,4096]{1,0:T(8,128)(2,1)} %second_ref.1) | copy-start | bytes 3145732
  11.6 7.7 %copy-start.19 = (s32[3]{0:T(128)S(1)}, s32[3]{0:T(128)}, u32[]{:S(2)}) copy-start(s32[3]{0:T(128)} %jobs_ref.1) | copy-start | bytes 40
  11.6 36.4 %all-to-all-start = ((bf16[16,24,1920]{2,1,0:T(8,128)(2,1)}), bf16[16,24,1920]{2,1,0:T(8,128)(2,1)S(1)}, u32[]{:S(2)}, u32[]{:S(2)}) async-start(bf16[16,24,1920]{2,1,0:T(8,128)(2,1)} %bitcast.1), calls=%async_computation | async-start | bytes 2949120 | tf_op jit(solution)/shard_map/all_to_all | solution.py:333
  19.4 1.0 copy-start.16
  21.4 13.4 %collective-permute-start.1 = (bf16[48,4224]{1,0:T(8,128)(2,1)S(1)}, bf16[48,4224]{1,0:T(8,128)(2,1)S(1)}, u32[]{:S(2)}, u32[]{:S(2)}) collective-permute-start(bf16[48,4224]{1,0:T(8,128)(2,1)S(1)} %shard_map.103.refs_3_), channel_id=1, source_target_pairs={{0,7},{1,0},{2,1},{3,2},{4,3},{5,4},{6,5},{7,6},{8,15},{9,8},{10,9... | collective-permute-start | bytes 1216520 | tf_op jit(solution)/shard_map/ppermute | solution.py:168
  27.0 11.0 %collective-permute-start = (bf16[48,4224]{1,0:T(8,128)(2,1)S(1)}, bf16[48,4224]{1,0:T(8,128)(2,1)S(1)}, u32[]{:S(2)}, u32[]{:S(2)}) collective-permute-start(bf16[48,4224]{1,0:T(8,128)(2,1)S(1)} %shard_map.103.refs_3_), channel_id=1, source_target_pairs={{0,1},{1,2},{2,3},{3,4},{4,5},{5,6},{6,7},{7,0},{8,9},{9,10},{10,1... | collective-permute-start | bytes 1216520 | tf_op jit(solution)/shard_map/ppermute | solution.py:168
  38.0 10.0 %collective-permute-start.2 = (bf16[48,4224]{1,0:T(8,128)(2,1)S(1)}, bf16[48,4224]{1,0:T(8,128)(2,1)S(1)}, u32[]{:S(2)}, u32[]{:S(2)}) collective-permute-start(bf16[48,4224]{1,0:T(8,128)(2,1)S(1)} %collective-permute-done.refs_2_), channel_id=1, source_target_pairs={{0,1},{1,2},{2,3},{3,4},{4,5},{5,6},{6,7},{7,0},{8,9},{9,10},{10,1... | collective-permute-start | bytes 1216520 | tf_op jit(solution)/shard_map/ppermute | solution.py:168
  38.0 0.7 copy-start.12
  38.7 9.3 %collective-permute-start.3 = (bf16[48,4224]{1,0:T(8,128)(2,1)S(1)}, bf16[48,4224]{1,0:T(8,128)(2,1)}, u32[]{:S(2)}, u32[]{:S(2)}) collective-permute-start(bf16[48,4224]{1,0:T(8,128)(2,1)S(1)} %collective-permute-done.1.refs_4_), channel_id=1, source_target_pairs={{0,7},{1,0},{2,1},{3,2},{4,3},{5,4},{6,5},{7,6},{8,15},{9,8},{10,9... | collective-permute-start | bytes 1216520 | tf_op jit(solution)/shard_map/ppermute | solution.py:168
  41.4 0.8 copy-start.10
  48.0 22.7 %collective-permute-start.4 = (bf16[384,1920]{1,0:T(8,128)(2,1)S(1)}, bf16[384,1920]{1,0:T(8,128)(2,1)}, u32[]{:S(2)}, u32[]{:S(2)}) collective-permute-start(bf16[384,1920]{1,0:T(8,128)(2,1)S(1)} %bitcast.38), channel_id=1, source_target_pairs={{0,8},{8,0},{16,24},{24,16},{32,40},{40,32},{48,56},{56,48},{64,72... | collective-permute-start | bytes 4423688 | tf_op jit(solution)/shard_map/ppermute | solution.py:27
  51.7 13.4 %collective-permute-start.8 = (bf16[48,4224]{1,0:T(8,128)(2,1)S(1)}, bf16[48,4224]{1,0:T(8,128)(2,1)S(1)}, u32[]{:S(2)}, u32[]{:S(2)}) collective-permute-start(bf16[48,4224]{1,0:T(8,128)(2,1)S(1)} %collective-permute-done.2.refs_1_), channel_id=1, source_target_pairs={{0,1},{1,2},{2,3},{3,4},{4,5},{5,6},{6,7},{7,0},{8,9},{9,10},{10,1... | collective-permute-start | bytes 1216520 | tf_op jit(solution)/shard_map/ppermute | solution.py:168
  51.7 0.8 copy-start.14
  52.4 12.6 %collective-permute-start.9 = (bf16[48,4224]{1,0:T(8,128)(2,1)}, bf16[48,4224]{1,0:T(8,128)(2,1)S(1)}, u32[]{:S(2)}, u32[]{:S(2)}) collective-permute-start(bf16[48,4224]{1,0:T(8,128)(2,1)} %collective-permute-done.3.refs_5_), channel_id=1, source_target_pairs={{0,7},{1,0},{2,1},{3,2},{4,3},{5,4},{6,5},{7,6},{8,15},{9,8},{10,9... | collective-permute-start | bytes 1216520 | tf_op jit(solution)/shard_map/ppermute | solution.py:168
  65.1 5.6 %copy-start.6 = (bf16[48,4224]{1,0:T(8,128)(2,1)}, bf16[48,4224]{1,0:T(8,128)(2,1)S(1)}, u32[]{:S(2)}) copy-start(bf16[48,4224]{1,0:T(8,128)(2,1)S(1)} %collective-permute-done.9.refs_6_) | copy-start | bytes 1216516
  65.8 0.7 copy-start.8
  66.6 12.8 %collective-permute-start.10 = (bf16[48,2048]{1,0:T(8,128)(2,1)}, bf16[48,2048]{1,0:T(8,128)(2,1)}, u32[]{:S(2)}, u32[]{:S(2)}) collective-permute-start(bf16[48,2048]{1,0:T(8,128)(2,1)} %slice.27), channel_id=1, source_target_pairs={{0,1},{1,2},{2,3},{3,4},{4,5},{5,6},{6,7},{7,0},{8,9},{9,10},{10,1... | collective-permute-start | bytes 589832 | tf_op jit(solution)/shard_map/ppermute | solution.py:168
  67.9 11.5 %collective-permute-start.11 = (bf16[48,2176]{1,0:T(8,128)(2,1)}, bf16[48,2176]{1,0:T(8,128)(2,1)S(1)}, u32[]{:S(2)}, u32[]{:S(2)}) collective-permute-start(bf16[48,2176]{1,0:T(8,128)(2,1)} %slice.28), channel_id=1, source_target_pairs={{0,7},{1,0},{2,1},{3,2},{4,3},{5,4},{6,5},{7,6},{8,15},{9,8},{10,9... | collective-permute-start | bytes 626696 | tf_op jit(solution)/shard_map/ppermute | solution.py:168
  73.8 5.5 %copy-start.7 = (bf16[48,4224]{1,0:T(8,128)(2,1)S(1)}, bf16[48,4224]{1,0:T(8,128)(2,1)}, u32[]{:S(2)}) copy-start(bf16[48,4224]{1,0:T(8,128)(2,1)} %copy-done.6) | copy-start | bytes 1216516
  73.8 5.5 %copy-start.9 = (bf16[48,4224]{1,0:T(8,128)(2,1)S(1)}, bf16[48,4224]{1,0:T(8,128)(2,1)}, u32[]{:S(2)}) copy-start(bf16[48,4224]{1,0:T(8,128)(2,1)} %copy-done.8) | copy-start | bytes 1216516
  73.9 5.5 %copy-start.11 = (bf16[48,4224]{1,0:T(8,128)(2,1)S(1)}, bf16[48,4224]{1,0:T(8,128)(2,1)}, u32[]{:S(2)}) copy-start(bf16[48,4224]{1,0:T(8,128)(2,1)} %copy-done.10) | copy-start | bytes 1216516
  75.8 3.1 %collective-permute-start.5 = (f32[16,384]{1,0:T(8,128)S(1)}, f32[16,384]{1,0:T(8,128)S(1)}, u32[]{:S(2)}, u32[]{:S(2)}) collective-permute-start(f32[16,384]{1,0:T(8,128)S(1)} %fusion.3), channel_id=1, source_target_pairs={{0,1},{1,0},{2,3},{3,2},{4,5},{5,4},{6,7},{7,6},{8,9},{9,8},{10,11... | collective-permute-start | bytes 73736 | tf_op jit(solution)/shard_map/ppermute | solution.py:200
  78.9 4.0 %collective-permute-start.6 = (f32[16,384]{1,0:T(8,128)S(1)}, f32[16,384]{1,0:T(8,128)S(1)}, u32[]{:S(2)}, u32[]{:S(2)}) collective-permute-start(f32[16,384]{1,0:T(8,128)S(1)} %add.113), channel_id=1, source_target_pairs={{0,2},{1,3},{2,0},{3,1},{4,6},{5,7},{6,4},{7,5},{8,10},{9,11},{10,... | collective-permute-start | bytes 73736 | tf_op jit(solution)/shard_map/ppermute | solution.py:200
  79.4 1.0 copy-start.13
  80.4 1.0 copy-start.15
  82.9 7.0 %copy-start.17 = (bf16[8,48,128]{2,1,0:T(8,128)(2,1)}, bf16[8,48,128]{2,1,0:T(8,128)(2,1)S(1)}, u32[]{:S(2)}) copy-start(bf16[8,48,128]{2,1,0:T(8,128)(2,1)S(1)} %get-tuple-element.42) | copy-start | bytes 294916
  82.9 7.0 %collective-permute-start.7 = (f32[16,384]{1,0:T(8,128)S(1)}, f32[16,384]{1,0:T(8,128)S(1)}, u32[]{:S(2)}, u32[]{:S(2)}) collective-permute-start(f32[16,384]{1,0:T(8,128)S(1)} %add.114), channel_id=1, source_target_pairs={{0,4},{1,5},{2,6},{3,7},{4,0},{5,1},{6,2},{7,3},{8,12},{9,13},{10,... | collective-permute-start | bytes 73736 | tf_op jit(solution)/shard_map/ppermute | solution.py:200
  91.1 1.6 copy-start.2
  92.7 22.0 %all-to-all-start.1 = ((bf16[32,72,128]{2,1,0:T(8,128)(2,1)}), bf16[32,72,128]{2,1,0:T(8,128)(2,1)S(1)}, u32[]{:S(2)}, u32[]{:S(2)}) async-start(bf16[32,72,128]{2,1,0:T(8,128)(2,1)} %shard_map.106), calls=%async_computation.1 | async-start | bytes 1179648 | tf_op jit(solution)/shard_map/all_to_all | solution.py:362
  102.5 59.8 %reduce-scatter.2.cloned.1.call-start = ((), (), s32[]{:S(2)}) async-start(), calls=%async_computation.5 | async-start | bytes 3538944 | tf_op jit(solution)/shard_map/reduce_scatter | solution.py:371
  111.7 1.6 copy-start.4
  114.9 2.5 %collective-permute-start.12 = (bf16[16,128]{1,0:T(8,128)(2,1)S(1)}, bf16[16,128]{1,0:T(8,128)(2,1)S(1)}, u32[]{:S(2)}, u32[]{:S(2)}) collective-permute-start(bf16[16,128]{1,0:T(8,128)(2,1)S(1)} %slice.34), channel_id=1, source_target_pairs={{0,1},{1,0},{2,3},{3,2},{4,5},{5,4},{6,7},{7,6},{8,9},{9,8},{10,11... | collective-permute-start | bytes 12296 | tf_op jit(solution)/shard_map/ppermute | solution.py:208
  117.5 3.4 %collective-permute-start.13 = (bf16[32,128]{1,0:T(8,128)(2,1)S(1)}, bf16[32,128]{1,0:T(8,128)(2,1)S(1)}, u32[]{:S(2)}, u32[]{:S(2)}) collective-permute-start(bf16[32,128]{1,0:T(8,128)(2,1)S(1)} %pad_maximum_fusion.2), channel_id=1, source_target_pairs={{0,2},{1,3},{2,0},{3,1},{4,6},{5,7},{6,4},{7,5},{8,10},{9,11},{10,... | collective-permute-start | bytes 24584 | tf_op jit(solution)/shard_map/ppermute | solution.py:208
  120.9 6.5 %collective-permute-start.14 = (bf16[64,128]{1,0:T(8,128)(2,1)S(1)}, bf16[64,128]{1,0:T(8,128)(2,1)S(1)}, u32[]{:S(2)}, u32[]{:S(2)}) collective-permute-start(bf16[64,128]{1,0:T(8,128)(2,1)S(1)} %pad_maximum_fusion.1), channel_id=1, source_target_pairs={{0,4},{1,5},{2,6},{3,7},{4,0},{5,1},{6,2},{7,3},{8,12},{9,13},{10,... | collective-permute-start | bytes 49160 | tf_op jit(solution)/shard_map/ppermute | solution.py:208
  128.7 9.8 %copy-start.18 = (bf16[8,48,128]{2,1,0:T(8,128)(2,1)S(1)}, bf16[8,48,128]{2,1,0:T(8,128)(2,1)}, u32[]{:S(2)}) copy-start(bf16[8,48,128]{2,1,0:T(8,128)(2,1)} %copy-done.17) | copy-start | bytes 294916
  128.7 9.8 %copy-start.20 = (bf16[1792,128]{1,0:T(8,128)(2,1)S(1)}, bf16[1792,128]{1,0:T(8,128)(2,1)}, u32[]{:S(2)}) copy-start(bf16[1792,128]{1,0:T(8,128)(2,1)} %first_ref.1) | copy-start | bytes 1376260
  128.7 31.7 %all-to-all-start.2 = ((bf16[32,184,128]{2,1,0:T(8,128)(2,1)}), bf16[32,184,128]{2,1,0:T(8,128)(2,1)S(1)}, u32[]{:S(2)}, u32[]{:S(2)}) async-start(bf16[32,184,128]{2,1,0:T(8,128)(2,1)} %broadcast_in_dim.39), calls=%async_computation.3 | async-start | bytes 3014656 | tf_op jit(solution)/shard_map/all_to_all | solution.py:367
  138.5 1.9 %copy-start.3 = (bf16[8,48,4096]{2,1,0:T(8,128)(2,1)S(1)}, bf16[8,48,4096]{2,1,0:T(8,128)(2,1)}, u32[]{:S(2)}) copy-start(bf16[8,48,4096]{2,1,0:T(8,128)(2,1)} %copy-done.2) | copy-start | bytes 9437188
  151.7 10.6 %copy-start.1 = (bf16[128,4096]{1,0:T(8,128)(2,1)S(1)}, bf16[128,4096]{1,0:T(8,128)(2,1)}, u32[]{:S(2)}) copy-start(bf16[128,4096]{1,0:T(8,128)(2,1)} %second_ref.1) | copy-start | bytes 3145732
Sparse Core Ops, SparseCore 0:
  11.1 84.4 all-gather.1
  114.9 42.5 reduce-scatter.1

commit v2 on v1

--- a/solution.py
+++ b/solution.py
@@ -13,6 +13,7 @@
 CHIPS = NX * NY
 LANES = 128
 VMEM_LIMIT = 40 * 1024 * 1024
+WHOLE_VMEM = 58 * 1024 * 1024
 F32 = jnp.float32
 BF16 = jnp.bfloat16
 
@@ -168,17 +169,20 @@
     return lax.ppermute(value, "tensor", [(i, (i + step) % NZ) for i in range(NZ)])
 
 
-def gather_z(piece, z):
+def gather_near(piece):
+    steps, up, down = [], piece, piece
+    for _ in range(1, NZ // 2):
+        up, down = lax.optimization_barrier((send_z(up, 1), send_z(down, -1)))
+        steps.append((up, down))
+    return steps
+
+
+def gather_far(piece, steps, last, z):
     rows, wide = piece.shape
     half = wide // (2 * LANES) * LANES
-    up = down = piece
-    pieces = [piece]
-    for step in range(1, NZ // 2):
-        up, down = lax.optimization_barrier((send_z(up, 1), send_z(down, -1)))
-        pieces = [up] + pieces + [down]
-        if step == 2:
-            between = (up, down)
-    pieces += lax.optimization_barrier((send_z(up[:, :half], 1), send_z(down[:, half:], -1)))
+    up, down = last
+    far = lax.optimization_barrier((send_z(up[:, :half], 1), send_z(down[:, half:], -1)))
+    pieces = [up for up, _ in steps[::-1]] + [piece] + [down for _, down in steps] + list(far)
     anywhere = pl.BlockSpec(memory_space=pl.ANY)
     model, inner = pl.pallas_call(
         functools.partial(order_kernel, half),
@@ -191,7 +195,7 @@
         scratch_shapes=[pltpu.SemaphoreType.DMA((2 * NZ + 1,))],
         compiler_params=params(),
     )(z.reshape(1), *pieces)
-    return model.reshape(NZ * rows, -1), inner.reshape(NZ * rows, LANES), between
+    return model.reshape(NZ * rows, -1), inner.reshape(NZ * rows, LANES)
 
 
 def sum_z(value):
@@ -211,14 +215,11 @@
     return value
 
 
-def share_kernel(z_ref, inner_ref, cot_ref, first_ref, out_ref):
+def share_kernel(_, inner_ref, cot_ref, first_ref, out_ref):
     parts, rows, _ = out_ref.shape
     firsts = first_ref.shape[0] // parts
     seconds = rows - firsts
-    wide = cot_ref.shape[1] // NZ
-    column = pl.multiple_of(z_ref[0] * wide, LANES)
-    block = ADAPTER_SCALE * dot_nn(inner_ref[...], cot_ref[:, pl.ds(column, wide)])
-    block = block.astype(BF16)
+    block = (ADAPTER_SCALE * dot_nn(inner_ref[...], cot_ref[...])).astype(BF16)
     each = block.shape[0] // seconds
     for i in range(parts):
         out_ref[i, :firsts, :] = first_ref[i * firsts : (i + 1) * firsts, :]
@@ -229,43 +230,54 @@
 def shares(z, inner, cotangent, first_part):
     parts = 2 * CHIPS
     rows = first_part.shape[0] // parts + inner.shape[0] * cotangent.shape[1] // (NZ * parts * LANES)
+    slots, model = cotangent.shape
     return pl.pallas_call(
         share_kernel,
         out_shape=jax.ShapeDtypeStruct((parts, rows, LANES), BF16),
-        in_specs=[SM, VM, VM, VM],
-        out_specs=VM,
-        compiler_params=params(),
+        grid_spec=pltpu.PrefetchScalarGridSpec(
+            num_scalar_prefetch=1,
+            grid=(1,),
+            in_specs=[
+                pl.BlockSpec(inner.shape, lambda i, z: (0, 0)),
+                pl.BlockSpec((slots, model // NZ), lambda i, z: (0, z[0])),
+                pl.BlockSpec(first_part.shape, lambda i, z: (0, 0)),
+            ],
+            out_specs=pl.BlockSpec((parts, rows, LANES), lambda i, z: (0, 0, 0)),
+        ),
+        compiler_params=params(WHOLE_VMEM),
     )(z.reshape(1), inner, cotangent, first_part)
 
 
-def finish_kernel(z_ref, every_ref, first_ref, second_ref):
-    parts, rows, _ = every_ref.shape
-    firsts = first_ref.shape[0] // parts
+def finish_kernel(place_ref, mine_ref, other_ref, first_ref, second_ref):
+    chips, rows, _ = mine_ref.shape
+    firsts = first_ref.shape[0] // (2 * chips)
     seconds = (rows - firsts) // NZ
     each = second_ref.shape[0] // seconds
     wide = second_ref.shape[1] // NZ
-    for i in range(parts):
-        first_ref[i * firsts : (i + 1) * firsts, :] = every_ref[i, :firsts, :].astype(F32)
-        share = every_ref[i, firsts:, :].astype(F32)
-        row = (i % each) * seconds
-        for place in range(NZ):
-            column = (z_ref[0] ^ place) * wide + (i // each) * LANES
-            second_ref[row : row + seconds, pl.ds(pl.multiple_of(column, LANES), LANES)] = share[
-                place * seconds : (place + 1) * seconds
-            ]
-
-
-def finish(z, every, units, width, model):
+    for core, part_ref in ((place_ref[1], mine_ref), (1 - place_ref[1], other_ref)):
+        for chip in range(chips):
+            spot = pl.multiple_of((2 * chip + core) * firsts, 8)
+            first_ref[pl.ds(spot, firsts), :] = part_ref[chip, :firsts, :].astype(F32)
+            share = part_ref[chip, firsts:, :].astype(F32)
+            row = pl.multiple_of(((2 * chip) % each + core) * seconds, 8)
+            for place in range(NZ):
+                column = (place_ref[0] ^ place) * wide + (2 * chip // each) * LANES
+                second_ref[pl.ds(row, seconds), pl.ds(pl.multiple_of(column, LANES), LANES)] = share[
+                    place * seconds : (place + 1) * seconds
+                ]
+
+
+def finish(z, core, mine, other, units, width, model):
     return pl.pallas_call(
         finish_kernel,
         out_shape=(
             jax.ShapeDtypeStruct((units, width), F32),
             jax.ShapeDtypeStruct((width, model), F32),
         ),
-        in_specs=[SM, VM],
+        in_specs=[SM, VM, VM],
         out_specs=(VM, VM),
         compiler_params=params(),
-    )(z.reshape(1), every)
+    )(jnp.stack([z, core]), mine, other)
 
 
 def forward_kernel(packed_ref, weight_ref, out_ref):
@@ -284,7 +296,7 @@
             pl.BlockSpec((tile, units), lambda i: (i, 0)),
         ],
         out_specs=pl.BlockSpec((slots, tile), lambda i: (0, i)),
-        compiler_params=params(),
+        compiler_params=params(WHOLE_VMEM),
         cost_estimate=pl.CostEstimate(
             flops=2 * slots * units * model,
             bytes_accessed=2 * (slots * units + units * model + slots * model),
@@ -312,7 +324,7 @@
             pl.BlockSpec((tile, LANES), lambda i: (i, 0)),
         ],
         out_specs=pl.BlockSpec((slots, tile), lambda i: (0, i)),
-        compiler_params=params(),
+        compiler_params=params(WHOLE_VMEM),
         cost_estimate=pl.CostEstimate(
             flops=2 * slots * units * model,
             bytes_accessed=2 * (slots * units + units * model + slots * model),
@@ -334,8 +346,8 @@
         sent, "dp", split_axis=0, concat_axis=0, axis_index_groups=SAME_CORE, tiled=True
     )
     piece = widen_cotangent(z, job_per_tile, cotangent, second_factors)
-    full_cotangent, inner_gradient, between = gather_z(piece, z)
-    got = after(got, *between)
+    steps = gather_near(piece)
+    got = after(got, *steps[1])
 
     packed = pack_rows(core, got, swap_core(got))
     slot_job = jnp.repeat(job_per_tile, rows // job_per_tile.shape[0], total_repeat_length=rows)
@@ -345,7 +357,9 @@
         slot_job[:, None] == column_job[None, :], dot_nn(packed, first_factors), 0.0
     ).astype(BF16)
     fold = (column[None, :] % ADAPTER_RANK == jnp.arange(ADAPTER_RANK)[:, None]).astype(BF16)
-    inner_sum = sum_z(dot_nt(fold, inner_part)).astype(BF16)
+    inner_part = dot_nt(fold, inner_part)
+    inner_sum = sum_z(inner_part).astype(BF16)
+    full_cotangent, inner_gradient = gather_far(piece, steps, after(steps[-1], inner_part), z)
     inner = jnp.where(
         slot_job[None, :] == column_job[:, None], jnp.tile(inner_sum, (width // ADAPTER_RANK, 1)), 0
     ).astype(BF16)
@@ -363,17 +377,19 @@
     share = jnp.sum(parts.astype(F32), axis=0).astype(BF16)
     firsts = units // (2 * CHIPS)
     share = jnp.concatenate([share[:firsts], gather_xor(share[firsts:])], axis=0)
-    spread = jnp.broadcast_to(share[None], (2 * CHIPS,) + share.shape)
-    every = lax.all_to_all(spread, "dp", split_axis=0, concat_axis=0, tiled=True)
+    spread = jnp.broadcast_to(share[None], (CHIPS,) + share.shape)
+    every = lax.all_to_all(
+        spread, "dp", split_axis=0, concat_axis=0, axis_index_groups=SAME_CORE, tiled=True
+    )
 
     weight = after(weight, sums)
     base = after(forward(packed, weight), parts)
     summed = lax.psum_scatter(base, "tensor", scatter_dimension=0, tiled=True)
     hidden_gradient = backward(full_cotangent, inner_gradient, weight, first_factors)
-    grad_a, second_gradient = finish(z, after(every, hidden_gradient), units, width, model)
-    mixed = (
-        summed.astype(F32) + ADAPTER_SCALE * dot_nn(my_inner, second_factors)
-    ).astype(BF16)
+    every = after(every, hidden_gradient)
+    grad_a, second_gradient = finish(z, core, every, swap_core(every), units, width, model)
+    adapted = lax.optimization_barrier(ADAPTER_SCALE * dot_nn(my_inner, second_factors))
+    mixed = (summed.astype(F32) + adapted).astype(BF16)
     return (mixed, hidden_gradient, grad_a, second_gradient)
 
 

time: 172 us -> 163 us (0.948)
  waiting for transfers between devices: 46.5 us -> 37.4 us
  local copies, waits for them, and re-layouts: 16.8 us -> 9.75 us
  Pallas kernels: 31.3 us -> 35.9 us
  other arithmetic: 2.23 us -> 4.73 us
    all_to_all x1, waiting for transfers between devices: 8.68 us -> 0.01 us  [on_device(): lax.all_to_all(spread, 'dp', split_axis=0, concat_axis=0, axis_index_grou...]
    unnamed x45 -> x29, local copies, waits for them, and re-layouts: 13.4 us -> 6.29 us
    all_to_all x1, starting transfers between devices: 9.75 us -> 4.84 us  [on_device(): lax.all_to_all(spread, 'dp', split_axis=0, concat_axis=0, axis_index_grou...]
    ppermute x8, waiting for transfers between devices: 23.9 us -> 19 us  [send_z(): lax.ppermute(value, 'tensor', [(i, (i + step) % NZ) for i in range(NZ)])]
    ppermute x1 -> x2, starting transfers between devices: 2.98 us -> 6.94 us  [swap_core(): return lax.ppermute(value, 'dp', [(i, i ^ 1) for i in range(2 * CHIPS)])]
    ppermute x3, starting transfers between devices: 3.49 us -> 6.54 us  [sum_z(): lax.ppermute(value, 'tensor', [(i, i ^ step) for i in range(NZ)])]
    ppermute x3, waiting for transfers between devices: 6.11 us -> 8.72 us  [gather_xor(): other = lax.ppermute(value, 'tensor', [(i, i ^ step) for i in range(NZ)])]
    ppermute x3, starting transfers between devices: 6.34 us -> 4.45 us  [gather_xor(): other = lax.ppermute(value, 'tensor', [(i, i ^ step) for i in range(NZ)])]
  transfers between devices with their start and end apart: 20 -> 21, of which waited for: 11 -> 13; matrix products, arithmetic and copies ran while one was open for 5% -> 6% of each run, Pallas kernels for 18% -> 22%
where the time goes in v2:
time: 163 us; the launch traced here: 161 us
  starting transfers between devices  54.9 us (34%)
  waiting for transfers between devices  37.4 us (23%)
  Pallas kernels  35.9 us (22%)
  between operations  14.3 us (9%)
  local copies, waits for them, and re-layouts  9.75 us (6%)
  other arithmetic  4.73 us (3%)
  matrix products  4.07 us (2%)
    ppermute x8, waiting for transfers between devices, send_z(): lax.ppermute(value, 'tensor', [(i, (i + step) % NZ) for i in range(NZ)])  19 us
    ppermute x8, starting transfers between devices, send_z(): lax.ppermute(value, 'tensor', [(i, (i + step) % NZ) for i in range(NZ)])  14.9 us
    pallas_call x1, Pallas kernels, backward(): pl.pallas_call(backward_kernel, grid=(units // tile,), out_shape=jax.Shap...  12.4 us
    pallas_call x1, Pallas kernels, forward(): pl.pallas_call(forward_kernel, grid=(model // tile,), out_shape=jax.Shape...  10.7 us
    all_to_all x1, starting transfers between devices, on_device(): parts = lax.all_to_all(sums, 'dp', split_axis=0, concat_axis=0, tiled=True)  9.41 us
    ppermute x3, waiting for transfers between devices, gather_xor(): other = lax.ppermute(value, 'tensor', [(i, i ^ step) for i in range(NZ)])  8.72 us
    all_to_all x1, starting transfers between devices, on_device(): lax.all_to_all(sent, 'dp', split_axis=0, concat_axis=0, axis_index_groups...  7.72 us
    ppermute x2, starting transfers between devices, swap_core(): return lax.ppermute(value, 'dp', [(i, i ^ 1) for i in range(2 * CHIPS)])  6.94 us
  transfers between devices with their start and end apart: 21, of which 13 were waited for; matrix products, arithmetic and copies ran while one was open for 6% of the time, Pallas kernels for 22%

profile of v2, /device:TPU:1, one launch (start us, length us, event | category | flops | bytes accessed | tf_op | source)
XLA Modules:
  0.0 161.1 jit_solution(17565908368324508093)
XLA Ops:
  7.2 2.1 %copy.11 = bf16[1792,128]{0,1:T(8,128)(2,1)} copy(bf16[1792,128]{1,0:T(8,128)(2,1)} %param.12) | data formatting | bytes 917504 | tf_op args[3]
  9.4 2.2 %shard_map.102 = bf16[384,1920]{1,0:T(8,128)(2,1)} custom-call(s32[1,384]{1,0:T(1,128)S(1)} %reshape.185.dest_ref, bf16[384,1792]{1,0:T(8,128)(2,1)S(1)} %copy-done.4), custom_call_target="tpu_custom_call" | custom-call | tf_op jit(solution)/shard_map/pallas_call | solution.py:80
  11.6 7.7 %all-to-all-start = ((bf16[16,24,1920]{2,1,0:T(8,128)(2,1)}), bf16[16,24,1920]{2,1,0:T(8,128)(2,1)S(1)}, u32[]{:S(2)}, u32[]{:S(2)}) async-start(bf16[16,24,1920]{2,1,0:T(8,128)(2,1)} %bitcast.1), calls=%async_computation | async-start | bytes 2949120 | tf_op jit(solution)/shard_map/all_to_all | solution.py:345
  19.4 1.0 copy-done.9
  20.4 1.0 shard_map.103.refs_3_
  21.4 5.7 %collective-permute-start.1 = (bf16[48,4224]{1,0:T(8,128)(2,1)S(1)}, bf16[48,4224]{1,0:T(8,128)(2,1)S(1)}, u32[]{:S(2)}, u32[]{:S(2)}) collective-permute-start(bf16[48,4224]{1,0:T(8,128)(2,1)S(1)} %shard_map.103.refs_3_), channel_id=1, source_target_pairs={{0,7},{1,0},{2,1},{3,2},{4,3},{5,4},{6,5},{7,6},{8,15},{9,8},{10,9... | collective-permute-start | bytes 1216520 | tf_op jit(solution)/shard_map/ppermute | solution.py:169
  27.1 7.7 %collective-permute-done.1.refs_4_ = bf16[48,4224]{1,0:T(8,128)(2,1)S(1)} collective-permute-done((bf16[48,4224]{1,0:T(8,128)(2,1)S(1)}, bf16[48,4224]{1,0:T(8,128)(2,1)S(1)}, u32[]{:S(2)}, u32[]{:S(2)}) %collective-permute-start.1) | collective-permute-done | bytes 405536 | tf_op jit(solution)/shard_map/ppermute | solution.py:169
  34.8 3.2 %collective-permute-done.refs_2_ = bf16[48,4224]{1,0:T(8,128)(2,1)S(1)} collective-permute-done((bf16[48,4224]{1,0:T(8,128)(2,1)S(1)}, bf16[48,4224]{1,0:T(8,128)(2,1)S(1)}, u32[]{:S(2)}, u32[]{:S(2)}) %collective-permute-start) | collective-permute-done | bytes 405536 | tf_op jit(solution)/shard_map/ppermute | solution.py:169
  38.0 0.7 copy-done.7
  38.8 2.7 %collective-permute-start.3 = (bf16[48,4224]{1,0:T(8,128)(2,1)S(1)}, bf16[48,4224]{1,0:T(8,128)(2,1)}, u32[]{:S(2)}, u32[]{:S(2)}) collective-permute-start(bf16[48,4224]{1,0:T(8,128)(2,1)S(1)} %collective-permute-done.1.refs_4_), channel_id=1, source_target_pairs={{0,7},{1,0},{2,1},{3,2},{4,3},{5,4},{6,5},{7,6},{8,15},{9,8},{10,9... | collective-permute-start | bytes 1216520 | tf_op jit(solution)/shard_map/ppermute | solution.py:169
  41.4 0.8 copy-done.5
  42.2 5.9 %collective-permute-done.2.refs_1_ = bf16[48,4224]{1,0:T(8,128)(2,1)} collective-permute-done((bf16[48,4224]{1,0:T(8,128)(2,1)S(1)}, bf16[48,4224]{1,0:T(8,128)(2,1)}, u32[]{:S(2)}, u32[]{:S(2)}) %collective-permute-start.2) | collective-permute-done | bytes 405536 | tf_op jit(solution)/shard_map/ppermute | solution.py:169
  48.1 3.0 %collective-permute-start.4 = (bf16[384,1920]{1,0:T(8,128)(2,1)S(1)}, bf16[384,1920]{1,0:T(8,128)(2,1)}, u32[]{:S(2)}, u32[]{:S(2)}) collective-permute-start(bf16[384,1920]{1,0:T(8,128)(2,1)S(1)} %bitcast.38), channel_id=1, source_target_pairs={{0,8},{8,0},{16,24},{24,16},{32,40},{40,32},{48,56},{56,48},{64,72... | collective-permute-start | bytes 4423688 | tf_op jit(solution)/shard_map/ppermute | solution.py:28
  51.1 0.6 fusion.18
  51.7 2.0 %fusion.16 = s32[384]{0:T(512)S(1)} fusion(s32[1,1,3,128]{3,2,1,0:T(4,128)S(1)} %get-tuple-element.56, s32[1,1,3,128]{3,2,1,0:T(4,128)S(1)} %get-tuple-element.55, s32[]{:T(128)} %bitcast.7, s32[]{:T(128)} %bitcast.9, s32[]{:T(128)} %bitcast.8), kind=kLoop, calls=%fused_computation.33 | loop fusion | flops 2304 | bytes 4620 | tf_op jit(solution)/shard_map/jit(_take)/gather | solution.py:353
  53.8 3.5 %collective-permute-start.9 = (bf16[48,4224]{1,0:T(8,128)(2,1)}, bf16[48,4224]{1,0:T(8,128)(2,1)}, u32[]{:S(2)}, u32[]{:S(2)}) collective-permute-start(bf16[48,4224]{1,0:T(8,128)(2,1)} %collective-permute-done.3.refs_5_), channel_id=1, source_target_pairs={{0,7},{1,0},{2,1},{3,2},{4,3},{5,4},{6,5},{7,6},{8,15},{9,8},{10,9... | collective-permute-start | bytes 1216520 | tf_op jit(solution)/shard_map/ppermute | solution.py:169
  57.3 3.1 %shard_map.104.packed_ref = bf16[384,1792]{1,0:T(8,128)(2,1)S(1)} custom-call(s32[1]{0:T(128)} %bitcast.core_ref, bf16[384,1920]{1,0:T(8,128)(2,1)S(1)} %bitcast.39, bf16[384,1920]{1,0:T(8,128)(2,1)} %collective-permute-done.4.other_ref), custom_call_target="tpu_custom_call" | custom-call | tf_op jit(solution)/shard_map/pallas_call | solution.py:109
  60.5 2.2 %fusion.1 = f32[16,384]{1,0:T(8,128)S(1)} fusion(bf16[384,1792]{1,0:T(8,128)(2,1)S(1)} %shard_map.104.packed_ref, bf16[1792,128]{1,0:T(8,128)(2,1)} %first_ref.1, s32[128]{0:T(128)S(1)} %and_select_fusion.1, s32[384]{0:T(512)S(1)} %and_select_fusion.2, s32[128]{0:T(128)S(1)} %and_select_fusion), kind=kOutput, calls=%fused_computation.4 | convolution fusion | flops 177883136 | bytes 1862144 | tf_op jit(solution)/shard_map/dot_general | solution.py:32
  62.7 3.2 %collective-permute-done.5 = f32[16,384]{1,0:T(8,128)S(1)} collective-permute-done((f32[16,384]{1,0:T(8,128)S(1)}, f32[16,384]{1,0:T(8,128)S(1)}, u32[]{:S(2)}, u32[]{:S(2)}) %collective-permute-start.5) | collective-permute-done | bytes 24608 | tf_op jit(solution)/shard_map/ppermute | solution.py:204
  65.8 2.5 %collective-permute-start.6 = (f32[16,384]{1,0:T(8,128)S(1)}, f32[16,384]{1,0:T(8,128)S(1)}, u32[]{:S(2)}, u32[]{:S(2)}) collective-permute-start(f32[16,384]{1,0:T(8,128)S(1)} %add.113), channel_id=1, source_target_pairs={{0,2},{1,3},{2,0},{3,1},{4,6},{5,7},{6,4},{7,5},{8,10},{9,11},{10,... | collective-permute-start | bytes 73736 | tf_op jit(solution)/shard_map/ppermute | solution.py:204
  68.3 1.9 %collective-permute-done.6 = f32[16,384]{1,0:T(8,128)S(1)} collective-permute-done((f32[16,384]{1,0:T(8,128)S(1)}, f32[16,384]{1,0:T(8,128)S(1)}, u32[]{:S(2)}, u32[]{:S(2)}) %collective-permute-start.6) | collective-permute-done | bytes 24608 | tf_op jit(solution)/shard_map/ppermute | solution.py:204
  70.2 4.1 %collective-permute-start.7 = (f32[16,384]{1,0:T(8,128)S(1)}, f32[16,384]{1,0:T(8,128)S(1)}, u32[]{:S(2)}, u32[]{:S(2)}) collective-permute-start(f32[16,384]{1,0:T(8,128)S(1)} %add.114), channel_id=1, source_target_pairs={{0,4},{1,5},{2,6},{3,7},{4,0},{5,1},{6,2},{7,3},{8,12},{9,13},{10,... | collective-permute-start | bytes 73736 | tf_op jit(solution)/shard_map/ppermute | solution.py:204
  74.3 1.0 slice.27
  75.3 0.9 slice.28
  76.3 2.9 %collective-permute-start.11 = (bf16[48,2176]{1,0:T(8,128)(2,1)S(1)}, bf16[48,2176]{1,0:T(8,128)(2,1)S(1)}, u32[]{:S(2)}, u32[]{:S(2)}) collective-permute-start(bf16[48,2176]{1,0:T(8,128)(2,1)S(1)} %slice.28), channel_id=1, source_target_pairs={{0,7},{1,0},{2,1},{3,2},{4,3},{5,4},{6,5},{7,6},{8,15},{9,8},{10,9... | collective-permute-start | bytes 626696 | tf_op jit(solution)/shard_map/ppermute | solution.py:169
  79.2 0.7 compare_select_fusion.inner_ref
  79.9 1.7 %collective-permute-done.10.refs_7_ = bf16[48,2048]{1,0:T(8,128)(2,1)S(1)} collective-permute-done((bf16[48,2048]{1,0:T(8,128)(2,1)S(1)}, bf16[48,2048]{1,0:T(8,128)(2,1)S(1)}, u32[]{:S(2)}, u32[]{:S(2)}) %collective-permute-start.10) | collective-permute-done | bytes 196640 | tf_op jit(solution)/shard_map/ppermute | solution.py:169
  82.1 1.6 %shard_map.105 = (bf16[8,48,4096]{2,1,0:T(8,128)(2,1)S(1)}, bf16[8,48,128]{2,1,0:T(8,128)(2,1)S(1)}) custom-call(s32[1]{0:T(128)} %bitcast.3.z_ref._, bf16[48,4224]{1,0:T(8,128)(2,1)} %collective-permute-done.8.refs_0_, bf16[48,4224]{1,0:T(8,128)(2,1)} %collective-permute-done.2.refs_1_, bf16[48,4224]{1,0:T(8,128)(2,1)S(1)} %copy-done.8, ...), custom_call_target="tpu_custom_call" | custom-call | tf_op jit(solution)/shard_map/pallas_call | solution.py:187
  83.7 1.6 %copy-done.3 = bf16[8,48,4096]{2,1,0:T(8,128)(2,1)} copy-done((bf16[8,48,4096]{2,1,0:T(8,128)(2,1)}, bf16[8,48,4096]{2,1,0:T(8,128)(2,1)S(1)}, u32[]{:S(2)}) %copy-start.3) | copy-done | bytes 3145752
  85.4 1.4 convolution_convert_fusion.first_ref
  86.7 2.2 %shard_map.106 = bf16[32,72,128]{2,1,0:T(8,128)(2,1)} custom-call(s32[1]{0:T(128)} %bitcast.3.z_ref._, bf16[128,384]{1,0:T(8,128)(2,1)} %compare_select_fusion.inner_ref, bf16[384,4096]{1,0:T(8,128)(2,1)} %bitcast.40, bf16[1792,128]{1,0:T(8,128)(2,1)} %convolution_convert_fusion.first_ref), custom_call_target="tpu_custom_call" | custom-call | tf_op jit(solution)/shard_map/pallas_call | solution.py:234
  89.0 9.4 %all-to-all-start.1 = ((bf16[32,72,128]{2,1,0:T(8,128)(2,1)}), bf16[32,72,128]{2,1,0:T(8,128)(2,1)S(1)}, u32[]{:S(2)}, u32[]{:S(2)}) async-start(bf16[32,72,128]{2,1,0:T(8,128)(2,1)} %shard_map.106), calls=%async_computation.1 | async-start | bytes 1179648 | tf_op jit(solution)/shard_map/all_to_all | solution.py:376
  98.5 10.7 %shard_map.107 = bf16[384,4096]{1,0:T(8,128)(2,1)} custom-call(bf16[384,1792]{1,0:T(8,128)(2,1)} %copy-done, bf16[4096,1792]{1,0:T(8,128)(2,1)} %all-gather.2.cloned.1.call-done.weight_ref), custom_call_target="tpu_custom_call" | custom-call | flops 5637144576 | bytes 19202048 | tf_op jit(solution)/shard_map/pallas_call | solution.py:290
  109.2 1.5 all-to-all-done.1
  110.8 1.9 %collective-permute-start.12 = (bf16[16,128]{1,0:T(8,128)(2,1)S(1)}, bf16[16,128]{1,0:T(8,128)(2,1)S(1)}, u32[]{:S(2)}, u32[]{:S(2)}) collective-permute-start(bf16[16,128]{1,0:T(8,128)(2,1)S(1)} %slice.34), channel_id=1, source_target_pairs={{0,1},{1,0},{2,3},{3,2},{4,5},{5,4},{6,7},{7,6},{8,9},{9,8},{10,11... | collective-permute-start | bytes 12296 | tf_op jit(solution)/shard_map/ppermute | solution.py:212
  112.7 1.2 collective-permute-done.12
  114.0 0.8 collective-permute-start.13
  114.8 2.6 %collective-permute-done.13 = bf16[32,128]{1,0:T(8,128)(2,1)S(1)} collective-permute-done((bf16[32,128]{1,0:T(8,128)(2,1)S(1)}, bf16[32,128]{1,0:T(8,128)(2,1)S(1)}, u32[]{:S(2)}, u32[]{:S(2)}) %collective-permute-start.13) | collective-permute-done | bytes 8224 | tf_op jit(solution)/shard_map/ppermute | solution.py:212
  117.4 1.7 %collective-permute-start.14 = (bf16[64,128]{1,0:T(8,128)(2,1)S(1)}, bf16[64,128]{1,0:T(8,128)(2,1)S(1)}, u32[]{:S(2)}, u32[]{:S(2)}) collective-permute-start(bf16[64,128]{1,0:T(8,128)(2,1)S(1)} %pad_maximum_fusion.1), channel_id=1, source_target_pairs={{0,4},{1,5},{2,6},{3,7},{4,0},{5,1},{6,2},{7,3},{8,12},{9,13},{10,... | collective-permute-start | bytes 49160 | tf_op jit(solution)/shard_map/ppermute | solution.py:212
  119.1 4.9 %collective-permute-done.14 = bf16[64,128]{1,0:T(8,128)(2,1)S(1)} collective-permute-done((bf16[64,128]{1,0:T(8,128)(2,1)S(1)}, bf16[64,128]{1,0:T(8,128)(2,1)S(1)}, u32[]{:S(2)}, u32[]{:S(2)}) %collective-permute-start.14) | collective-permute-done | bytes 16416 | tf_op jit(solution)/shard_map/ppermute | solution.py:212
  124.0 1.0 broadcast_in_dim.39
  125.0 4.8 %all-to-all-start.2 = ((bf16[16,184,128]{2,1,0:T(8,128)(2,1)}), bf16[16,184,128]{2,1,0:T(8,128)(2,1)S(1)}, u32[]{:S(2)}, u32[]{:S(2)}) async-start(bf16[16,184,128]{2,1,0:T(8,128)(2,1)} %broadcast_in_dim.39), calls=%async_computation.3 | async-start | bytes 1507328 | tf_op jit(solution)/shard_map/all_to_all | solution.py:381
  129.8 12.4 %shard_map.108 = bf16[384,1792]{1,0:T(8,128)(2,1)} custom-call(bf16[384,4096]{1,0:T(8,128)(2,1)} %bitcast.41, bf16[384,128]{1,0:T(8,128)(2,1)} %bitcast.43, bf16[4096,1792]{1,0:T(8,128)(2,1)} %all-gather.2.cloned.1.call-done.weight_ref, bf16[1792,128]{1,0:T(8,128)(2,1)} %first_ref.1), custom_call_target="tpu_custom_call" | custom-call | flops 5637144576 | bytes 19202048 | tf_op jit(solution)/shard_map/pallas_call | solution.py:316
  142.2 4.0 %collective-permute-start.15 = (bf16[16,184,128]{2,1,0:T(8,128)(2,1)S(1)}, bf16[16,184,128]{2,1,0:T(8,128)(2,1)S(1)}, u32[]{:S(2)}, u32[]{:S(2)}) collective-permute-start(bf16[16,184,128]{2,1,0:T(8,128)(2,1)S(1)} %all-to-all-done.2.mine_ref), channel_id=1, source_target_pairs={{0,8},{8,0},{16,24},{24,16},{32,40},{40,32},{48,56},{56,48},{64,72... | collective-permute-start | bytes 2261000 | tf_op jit(solution)/shard_map/ppermute | solution.py:28
  146.8 1.3 collective-permute-done.15.other_ref
  148.1 2.5 %shard_map.109 = (f32[1792,128]{1,0:T(8,128)}, f32[128,4096]{1,0:T(8,128)}) custom-call(s32[2]{0:T(128)S(1)} %pad_add_fusion.place_ref, bf16[16,184,128]{2,1,0:T(8,128)(2,1)S(1)} %all-to-all-done.2.mine_ref, bf16[16,184,128]{2,1,0:T(8,128)(2,1)S(1)} %collective-permute-done.15.other_ref), custom_call_target="tpu_custom_call" | custom-call | tf_op jit(solution)/shard_map/pallas_call | solution.py:271
  150.6 1.8 %reduce-scatter.2.cloned.1.call-done = bf16[48,4096]{1,0:T(8,128)(2,1)} async-done(((bf16[384,4096]{1,0:T(8,128)(2,1)}), bf16[48,4096]{1,0:T(8,128)(2,1)}) %reduce-scatter.2.cloned.1.call-update) | async-done | bytes 393232 | tf_op jit(solution)/shard_map/reduce_scatter | solution.py:387
  152.4 1.8 %add_convert_fusion = bf16[48,4096]{1,0:T(8,128)(2,1)} fusion(f32[48,4096]{1,0:T(8,128)S(1)} %convolution_multiply_fusion, bf16[48,4096]{1,0:T(8,128)(2,1)} %reduce-scatter.2.cloned.1.call-done), kind=kLoop, calls=%fused_computation.6 | loop fusion | flops 589824 | bytes 1572864 | tf_op jit(solution)/shard_map/convert_element_type | solution.py:392
  (58 shorter events, 1.6 us)
Async XLA Ops:
  7.2 2.2 %copy-start.13 = (s32[384]{0:T(512)S(1)}, s32[384]{0:T(512)}, u32[]{:S(2)}) copy-start(s32[384]{0:T(512)} %param.10) | copy-start | bytes 4612
  7.2 2.2 %copy-start.4 = (bf16[384,1792]{1,0:T(8,128)(2,1)S(1)}, bf16[384,1792]{1,0:T(8,128)(2,1)}, u32[]{:S(2)}) copy-start(bf16[384,1792]{1,0:T(8,128)(2,1)} %hidden_ref.1) | copy-start | bytes 4128772
  7.2 91.3 %all-gather.2.cloned.1.call-start = ((), (), s32[]{:S(2)}) async-start(), calls=%async_computation.4 | async-start | bytes 15138816 | tf_op jit(solution)/shard_map/all_gather | solution.py:343
  11.6 7.7 %copy-start.1 = (bf16[128,4096]{1,0:T(8,128)(2,1)S(1)}, bf16[128,4096]{1,0:T(8,128)(2,1)}, u32[]{:S(2)}) copy-start(bf16[128,4096]{1,0:T(8,128)(2,1)} %second_ref.1) | copy-start | bytes 3145732
  11.6 7.7 %copy-start.11 = (s32[3]{0:T(128)S(1)}, s32[3]{0:T(128)}, u32[]{:S(2)}) copy-start(s32[3]{0:T(128)} %jobs_ref.1) | copy-start | bytes 40
  11.6 36.5 %all-to-all-start = ((bf16[16,24,1920]{2,1,0:T(8,128)(2,1)}), bf16[16,24,1920]{2,1,0:T(8,128)(2,1)S(1)}, u32[]{:S(2)}, u32[]{:S(2)}) async-start(bf16[16,24,1920]{2,1,0:T(8,128)(2,1)} %bitcast.1), calls=%async_computation | async-start | bytes 2949120 | tf_op jit(solution)/shard_map/all_to_all | solution.py:345
  19.4 1.0 copy-start.9
  21.4 13.4 %collective-permute-start.1 = (bf16[48,4224]{1,0:T(8,128)(2,1)S(1)}, bf16[48,4224]{1,0:T(8,128)(2,1)S(1)}, u32[]{:S(2)}, u32[]{:S(2)}) collective-permute-start(bf16[48,4224]{1,0:T(8,128)(2,1)S(1)} %shard_map.103.refs_3_), channel_id=1, source_target_pairs={{0,7},{1,0},{2,1},{3,2},{4,3},{5,4},{6,5},{7,6},{8,15},{9,8},{10,9... | collective-permute-start | bytes 1216520 | tf_op jit(solution)/shard_map/ppermute | solution.py:169
  27.0 10.9 %collective-permute-start = (bf16[48,4224]{1,0:T(8,128)(2,1)S(1)}, bf16[48,4224]{1,0:T(8,128)(2,1)S(1)}, u32[]{:S(2)}, u32[]{:S(2)}) collective-permute-start(bf16[48,4224]{1,0:T(8,128)(2,1)S(1)} %shard_map.103.refs_3_), channel_id=1, source_target_pairs={{0,1},{1,2},{2,3},{3,4},{4,5},{5,6},{6,7},{7,0},{8,9},{9,10},{10,1... | collective-permute-start | bytes 1216520 | tf_op jit(solution)/shard_map/ppermute | solution.py:169
  38.0 10.1 %collective-permute-start.2 = (bf16[48,4224]{1,0:T(8,128)(2,1)S(1)}, bf16[48,4224]{1,0:T(8,128)(2,1)}, u32[]{:S(2)}, u32[]{:S(2)}) collective-permute-start(bf16[48,4224]{1,0:T(8,128)(2,1)S(1)} %collective-permute-done.refs_2_), channel_id=1, source_target_pairs={{0,1},{1,2},{2,3},{3,4},{4,5},{5,6},{6,7},{7,0},{8,9},{9,10},{10,1... | collective-permute-start | bytes 1216520 | tf_op jit(solution)/shard_map/ppermute | solution.py:169
  38.0 0.8 copy-start.7
  38.8 9.4 %collective-permute-start.3 = (bf16[48,4224]{1,0:T(8,128)(2,1)S(1)}, bf16[48,4224]{1,0:T(8,128)(2,1)}, u32[]{:S(2)}, u32[]{:S(2)}) collective-permute-start(bf16[48,4224]{1,0:T(8,128)(2,1)S(1)} %collective-permute-done.1.refs_4_), channel_id=1, source_target_pairs={{0,7},{1,0},{2,1},{3,2},{4,3},{5,4},{6,5},{7,6},{8,15},{9,8},{10,9... | collective-permute-start | bytes 1216520 | tf_op jit(solution)/shard_map/ppermute | solution.py:169
  41.4 0.8 copy-start.5
  48.1 9.1 %collective-permute-start.4 = (bf16[384,1920]{1,0:T(8,128)(2,1)S(1)}, bf16[384,1920]{1,0:T(8,128)(2,1)}, u32[]{:S(2)}, u32[]{:S(2)}) collective-permute-start(bf16[384,1920]{1,0:T(8,128)(2,1)S(1)} %bitcast.38), channel_id=1, source_target_pairs={{0,8},{8,0},{16,24},{24,16},{32,40},{40,32},{48,56},{56,48},{64,72... | collective-permute-start | bytes 4423688 | tf_op jit(solution)/shard_map/ppermute | solution.py:28
  53.7 20.6 %collective-permute-start.8 = (bf16[48,4224]{1,0:T(8,128)(2,1)}, bf16[48,4224]{1,0:T(8,128)(2,1)}, u32[]{:S(2)}, u32[]{:S(2)}) collective-permute-start(bf16[48,4224]{1,0:T(8,128)(2,1)} %collective-permute-done.2.refs_1_), channel_id=1, source_target_pairs={{0,1},{1,2},{2,3},{3,4},{4,5},{5,6},{6,7},{7,0},{8,9},{9,10},{10,1... | collective-permute-start | bytes 1216520 | tf_op jit(solution)/shard_map/ppermute | solution.py:169
  53.8 20.5 %collective-permute-start.9 = (bf16[48,4224]{1,0:T(8,128)(2,1)}, bf16[48,4224]{1,0:T(8,128)(2,1)}, u32[]{:S(2)}, u32[]{:S(2)}) collective-permute-start(bf16[48,4224]{1,0:T(8,128)(2,1)} %collective-permute-done.3.refs_5_), channel_id=1, source_target_pairs={{0,7},{1,0},{2,1},{3,2},{4,3},{5,4},{6,5},{7,6},{8,15},{9,8},{10,9... | collective-permute-start | bytes 1216520 | tf_op jit(solution)/shard_map/ppermute | solution.py:169
  60.4 25.0 %copy-start = (bf16[384,1792]{1,0:T(8,128)(2,1)}, bf16[384,1792]{1,0:T(8,128)(2,1)S(1)}, u32[]{:S(2)}) copy-start(bf16[384,1792]{1,0:T(8,128)(2,1)S(1)} %shard_map.104.packed_ref) | copy-start | bytes 4128772
  60.4 21.6 %copy-start.6 = (bf16[48,4224]{1,0:T(8,128)(2,1)S(1)}, bf16[48,4224]{1,0:T(8,128)(2,1)}, u32[]{:S(2)}) copy-start(bf16[48,4224]{1,0:T(8,128)(2,1)} %copy-done.5) | copy-start | bytes 1216516
  60.4 21.6 %copy-start.8 = (bf16[48,4224]{1,0:T(8,128)(2,1)S(1)}, bf16[48,4224]{1,0:T(8,128)(2,1)}, u32[]{:S(2)}) copy-start(bf16[48,4224]{1,0:T(8,128)(2,1)} %copy-done.7) | copy-start | bytes 1216516
  62.7 3.2 %collective-permute-start.5 = (f32[16,384]{1,0:T(8,128)S(1)}, f32[16,384]{1,0:T(8,128)S(1)}, u32[]{:S(2)}, u32[]{:S(2)}) collective-permute-start(f32[16,384]{1,0:T(8,128)S(1)} %fusion.1), channel_id=1, source_target_pairs={{0,1},{1,0},{2,3},{3,2},{4,5},{5,4},{6,7},{7,6},{8,9},{9,8},{10,11... | collective-permute-start | bytes 73736 | tf_op jit(solution)/shard_map/ppermute | solution.py:204
  65.8 4.3 %collective-permute-start.6 = (f32[16,384]{1,0:T(8,128)S(1)}, f32[16,384]{1,0:T(8,128)S(1)}, u32[]{:S(2)}, u32[]{:S(2)}) collective-permute-start(f32[16,384]{1,0:T(8,128)S(1)} %add.113), channel_id=1, source_target_pairs={{0,2},{1,3},{2,0},{3,1},{4,6},{5,7},{6,4},{7,5},{8,10},{9,11},{10,... | collective-permute-start | bytes 73736 | tf_op jit(solution)/shard_map/ppermute | solution.py:204
  70.2 9.0 %collective-permute-start.7 = (f32[16,384]{1,0:T(8,128)S(1)}, f32[16,384]{1,0:T(8,128)S(1)}, u32[]{:S(2)}, u32[]{:S(2)}) collective-permute-start(f32[16,384]{1,0:T(8,128)S(1)} %add.114), channel_id=1, source_target_pairs={{0,4},{1,5},{2,6},{3,7},{4,0},{5,1},{6,2},{7,3},{8,12},{9,13},{10,... | collective-permute-start | bytes 73736 | tf_op jit(solution)/shard_map/ppermute | solution.py:204
  75.2 6.4 %collective-permute-start.10 = (bf16[48,2048]{1,0:T(8,128)(2,1)S(1)}, bf16[48,2048]{1,0:T(8,128)(2,1)S(1)}, u32[]{:S(2)}, u32[]{:S(2)}) collective-permute-start(bf16[48,2048]{1,0:T(8,128)(2,1)S(1)} %slice.27), channel_id=1, source_target_pairs={{0,1},{1,2},{2,3},{3,4},{4,5},{5,6},{6,7},{7,0},{8,9},{9,10},{10,1... | collective-permute-start | bytes 589832 | tf_op jit(solution)/shard_map/ppermute | solution.py:169
  76.3 5.8 %collective-permute-start.11 = (bf16[48,2176]{1,0:T(8,128)(2,1)S(1)}, bf16[48,2176]{1,0:T(8,128)(2,1)S(1)}, u32[]{:S(2)}, u32[]{:S(2)}) collective-permute-start(bf16[48,2176]{1,0:T(8,128)(2,1)S(1)} %slice.28), channel_id=1, source_target_pairs={{0,7},{1,0},{2,1},{3,2},{4,3},{5,4},{6,5},{7,6},{8,15},{9,8},{10,9... | collective-permute-start | bytes 626696 | tf_op jit(solution)/shard_map/ppermute | solution.py:169
  83.7 1.6 %copy-start.3 = (bf16[8,48,4096]{2,1,0:T(8,128)(2,1)}, bf16[8,48,4096]{2,1,0:T(8,128)(2,1)S(1)}, u32[]{:S(2)}) copy-start(bf16[8,48,4096]{2,1,0:T(8,128)(2,1)S(1)} %get-tuple-element.45) | copy-start | bytes 9437188
  85.4 3.6 %copy-start.10 = (bf16[8,48,128]{2,1,0:T(8,128)(2,1)}, bf16[8,48,128]{2,1,0:T(8,128)(2,1)S(1)}, u32[]{:S(2)}) copy-start(bf16[8,48,128]{2,1,0:T(8,128)(2,1)S(1)} %get-tuple-element.46) | copy-start | bytes 294916
  89.0 21.7 %all-to-all-start.1 = ((bf16[32,72,128]{2,1,0:T(8,128)(2,1)}), bf16[32,72,128]{2,1,0:T(8,128)(2,1)S(1)}, u32[]{:S(2)}, u32[]{:S(2)}) async-start(bf16[32,72,128]{2,1,0:T(8,128)(2,1)} %shard_map.106), calls=%async_computation.1 | async-start | bytes 1179648 | tf_op jit(solution)/shard_map/all_to_all | solution.py:376
  98.4 54.0 %reduce-scatter.2.cloned.1.call-start = ((), (), s32[]{:S(2)}) async-start(), calls=%async_computation.5 | async-start | bytes 3538944 | tf_op jit(solution)/shard_map/reduce_scatter | solution.py:387
  110.8 3.2 %collective-permute-start.12 = (bf16[16,128]{1,0:T(8,128)(2,1)S(1)}, bf16[16,128]{1,0:T(8,128)(2,1)S(1)}, u32[]{:S(2)}, u32[]{:S(2)}) collective-permute-start(bf16[16,128]{1,0:T(8,128)(2,1)S(1)} %slice.34), channel_id=1, source_target_pairs={{0,1},{1,0},{2,3},{3,2},{4,5},{5,4},{6,7},{7,6},{8,9},{9,8},{10,11... | collective-permute-start | bytes 12296 | tf_op jit(solution)/shard_map/ppermute | solution.py:212
  114.0 3.4 %collective-permute-start.13 = (bf16[32,128]{1,0:T(8,128)(2,1)S(1)}, bf16[32,128]{1,0:T(8,128)(2,1)S(1)}, u32[]{:S(2)}, u32[]{:S(2)}) collective-permute-start(bf16[32,128]{1,0:T(8,128)(2,1)S(1)} %pad_maximum_fusion.2), channel_id=1, source_target_pairs={{0,2},{1,3},{2,0},{3,1},{4,6},{5,7},{6,4},{7,5},{8,10},{9,11},{10,... | collective-permute-start | bytes 24584 | tf_op jit(solution)/shard_map/ppermute | solution.py:212
  117.4 6.6 %collective-permute-start.14 = (bf16[64,128]{1,0:T(8,128)(2,1)S(1)}, bf16[64,128]{1,0:T(8,128)(2,1)S(1)}, u32[]{:S(2)}, u32[]{:S(2)}) collective-permute-start(bf16[64,128]{1,0:T(8,128)(2,1)S(1)} %pad_maximum_fusion.1), channel_id=1, source_target_pairs={{0,4},{1,5},{2,6},{3,7},{4,0},{5,1},{6,2},{7,3},{8,12},{9,13},{10,... | collective-permute-start | bytes 49160 | tf_op jit(solution)/shard_map/ppermute | solution.py:212
  125.0 17.3 %all-to-all-start.2 = ((bf16[16,184,128]{2,1,0:T(8,128)(2,1)}), bf16[16,184,128]{2,1,0:T(8,128)(2,1)S(1)}, u32[]{:S(2)}, u32[]{:S(2)}) async-start(bf16[16,184,128]{2,1,0:T(8,128)(2,1)} %broadcast_in_dim.39), calls=%async_computation.3 | async-start | bytes 1507328 | tf_op jit(solution)/shard_map/all_to_all | solution.py:381
  129.8 16.5 %copy-start.2 = (bf16[128,4096]{1,0:T(8,128)(2,1)S(1)}, bf16[128,4096]{1,0:T(8,128)(2,1)}, u32[]{:S(2)}) copy-start(bf16[128,4096]{1,0:T(8,128)(2,1)} %second_ref.1) | copy-start | bytes 3145732
  129.8 16.5 %copy-start.12 = (bf16[128,384]{1,0:T(8,128)(2,1)S(1)}, bf16[128,384]{1,0:T(8,128)(2,1)}, u32[]{:S(2)}) copy-start(bf16[128,384]{1,0:T(8,128)(2,1)} %compare_select_fusion.inner_ref) | copy-start | bytes 294916
  142.2 5.8 %collective-permute-start.15 = (bf16[16,184,128]{2,1,0:T(8,128)(2,1)S(1)}, bf16[16,184,128]{2,1,0:T(8,128)(2,1)S(1)}, u32[]{:S(2)}, u32[]{:S(2)}) collective-permute-start(bf16[16,184,128]{2,1,0:T(8,128)(2,1)S(1)} %all-to-all-done.2.mine_ref), channel_id=1, source_target_pairs={{0,8},{8,0},{16,24},{24,16},{32,40},{40,32},{48,56},{56,48},{64,72... | collective-permute-start | bytes 2261000 | tf_op jit(solution)/shard_map/ppermute | solution.py:28
Sparse Core Ops, SparseCore 0:
  10.6 85.0 all-gather.1
  110.8 41.5 reduce-scatter.1

commit v3 on v2

--- a/solution.py
+++ b/solution.py
@@ -177,11 +177,16 @@
     return steps
 
 
-def gather_far(piece, steps, last, z):
+def last_parts(last):
+    up, down = last
+    half = up.shape[1] // (2 * LANES) * LANES
+    return lax.optimization_barrier((up[:, :half], down[:, half:]))
+
+
+def gather_far(piece, steps, parts, z):
     rows, wide = piece.shape
-    half = wide // (2 * LANES) * LANES
-    up, down = last
-    far = lax.optimization_barrier((send_z(up[:, :half], 1), send_z(down[:, half:], -1)))
+    half = parts[0].shape[1]
+    far = lax.optimization_barrier((send_z(parts[0], 1), send_z(parts[1], -1)))
     pieces = [up for up, _ in steps[::-1]] + [piece] + [down for _, down in steps] + list(far)
     anywhere = pl.BlockSpec(memory_space=pl.ANY)
     model, inner = pl.pallas_call(
@@ -198,9 +203,11 @@
     return model.reshape(NZ * rows, -1), inner.reshape(NZ * rows, LANES)
 
 
-def sum_z(value):
+def sum_z(value, hold):
     step = 1
     while step < NZ:
+        if 2 * step == NZ:
+            value = after(value, *hold)
         value = value + lax.ppermute(value, "tensor", [(i, i ^ step) for i in range(NZ)])
         step *= 2
     return value
@@ -358,8 +365,9 @@
     ).astype(BF16)
     fold = (column[None, :] % ADAPTER_RANK == jnp.arange(ADAPTER_RANK)[:, None]).astype(BF16)
     inner_part = dot_nt(fold, inner_part)
-    inner_sum = sum_z(inner_part).astype(BF16)
-    full_cotangent, inner_gradient = gather_far(piece, steps, after(steps[-1], inner_part), z)
+    opposite = last_parts(after(steps[-1], inner_part))
+    inner_sum = sum_z(inner_part, opposite).astype(BF16)
+    full_cotangent, inner_gradient = gather_far(piece, steps, opposite, z)
     inner = jnp.where(
         slot_job[None, :] == column_job[:, None], jnp.tile(inner_sum, (width // ADAPTER_RANK, 1)), 0
     ).astype(BF16)

time: 163 us -> 162 us (level)
  waiting for transfers between devices: 37.4 us -> 35.7 us
    ppermute x3, waiting for transfers between devices: 5.03 us -> 3.25 us  [sum_z(): lax.ppermute(value, 'tensor', [(i, i ^ step) for i in range(NZ)])]
  transfers between devices with their start and end apart: 21 -> 21, of which waited for: 13 -> 12; matrix products, arithmetic and copies ran while one was open for 6% -> 7% of each run, Pallas kernels for 22% -> 23%
where the time goes in v3:
time: 162 us; the launch traced here: 159 us
  starting transfers between devices  54.4 us (34%)
  Pallas kernels  36.2 us (22%)
  waiting for transfers between devices  35.7 us (22%)
  between operations  14.3 us (9%)
  local copies, waits for them, and re-layouts  9.75 us (6%)
  other arithmetic  4.73 us (3%)
  matrix products  4.07 us (3%)
    ppermute x8, waiting for transfers between devices, send_z(): lax.ppermute(value, 'tensor', [(i, (i + step) % NZ) for i in range(NZ)])  20.4 us
    ppermute x8, starting transfers between devices, send_z(): lax.ppermute(value, 'tensor', [(i, (i + step) % NZ) for i in range(NZ)])  14.6 us
    pallas_call x1, Pallas kernels, backward(): pl.pallas_call(backward_kernel, grid=(units // tile,), out_shape=jax.Shap...  12.4 us
    pallas_call x1, Pallas kernels, forward(): pl.pallas_call(forward_kernel, grid=(model // tile,), out_shape=jax.Shape...  10.7 us
    all_to_all x1, starting transfers between devices, on_device(): parts = lax.all_to_all(sums, 'dp', split_axis=0, concat_axis=0, tiled=True)  8.23 us
    all_to_all x1, starting transfers between devices, on_device(): lax.all_to_all(sent, 'dp', split_axis=0, concat_axis=0, axis_index_groups...  7.72 us
    ppermute x3, waiting for transfers between devices, gather_xor(): other = lax.ppermute(value, 'tensor', [(i, i ^ step) for i in range(NZ)])  7.51 us
    ppermute x2, starting transfers between devices, swap_core(): return lax.ppermute(value, 'dp', [(i, i ^ 1) for i in range(2 * CHIPS)])  7.16 us
  transfers between devices with their start and end apart: 21, of which 12 were waited for; matrix products, arithmetic and copies ran while one was open for 7% of the time, Pallas kernels for 23%

profile of v3, /device:TPU:1, one launch (start us, length us, event | category | flops | bytes accessed | tf_op | source)
XLA Modules:
  0.0 159.2 jit_solution(4181762602276201363)
XLA Ops:
  7.2 2.1 %copy.11 = bf16[1792,128]{0,1:T(8,128)(2,1)} copy(bf16[1792,128]{1,0:T(8,128)(2,1)} %param.12) | data formatting | bytes 917504 | tf_op args[3]
  9.4 2.2 %shard_map.102 = bf16[384,1920]{1,0:T(8,128)(2,1)} custom-call(s32[1,384]{1,0:T(1,128)S(1)} %reshape.185.dest_ref, bf16[384,1792]{1,0:T(8,128)(2,1)S(1)} %copy-done.4), custom_call_target="tpu_custom_call" | custom-call | tf_op jit(solution)/shard_map/pallas_call | solution.py:80
  11.6 7.7 %all-to-all-start = ((bf16[16,24,1920]{2,1,0:T(8,128)(2,1)}), bf16[16,24,1920]{2,1,0:T(8,128)(2,1)S(1)}, u32[]{:S(2)}, u32[]{:S(2)}) async-start(bf16[16,24,1920]{2,1,0:T(8,128)(2,1)} %bitcast.1), calls=%async_computation | async-start | bytes 2949120 | tf_op jit(solution)/shard_map/all_to_all | solution.py:352
  19.4 1.0 copy-done.9
  20.4 1.0 shard_map.103.refs_3_
  21.4 5.7 %collective-permute-start.1 = (bf16[48,4224]{1,0:T(8,128)(2,1)S(1)}, bf16[48,4224]{1,0:T(8,128)(2,1)S(1)}, u32[]{:S(2)}, u32[]{:S(2)}) collective-permute-start(bf16[48,4224]{1,0:T(8,128)(2,1)S(1)} %shard_map.103.refs_3_), channel_id=1, source_target_pairs={{0,7},{1,0},{2,1},{3,2},{4,3},{5,4},{6,5},{7,6},{8,15},{9,8},{10,9... | collective-permute-start | bytes 1216520 | tf_op jit(solution)/shard_map/ppermute | solution.py:169
  27.1 7.7 %collective-permute-done.1.refs_4_ = bf16[48,4224]{1,0:T(8,128)(2,1)S(1)} collective-permute-done((bf16[48,4224]{1,0:T(8,128)(2,1)S(1)}, bf16[48,4224]{1,0:T(8,128)(2,1)S(1)}, u32[]{:S(2)}, u32[]{:S(2)}) %collective-permute-start.1) | collective-permute-done | bytes 405536 | tf_op jit(solution)/shard_map/ppermute | solution.py:169
  34.8 3.2 %collective-permute-done.refs_2_ = bf16[48,4224]{1,0:T(8,128)(2,1)S(1)} collective-permute-done((bf16[48,4224]{1,0:T(8,128)(2,1)S(1)}, bf16[48,4224]{1,0:T(8,128)(2,1)S(1)}, u32[]{:S(2)}, u32[]{:S(2)}) %collective-permute-start) | collective-permute-done | bytes 405536 | tf_op jit(solution)/shard_map/ppermute | solution.py:169
  38.0 0.7 copy-done.7
  38.8 2.7 %collective-permute-start.3 = (bf16[48,4224]{1,0:T(8,128)(2,1)S(1)}, bf16[48,4224]{1,0:T(8,128)(2,1)}, u32[]{:S(2)}, u32[]{:S(2)}) collective-permute-start(bf16[48,4224]{1,0:T(8,128)(2,1)S(1)} %collective-permute-done.1.refs_4_), channel_id=1, source_target_pairs={{0,7},{1,0},{2,1},{3,2},{4,3},{5,4},{6,5},{7,6},{8,15},{9,8},{10,9... | collective-permute-start | bytes 1216520 | tf_op jit(solution)/shard_map/ppermute | solution.py:169
  41.4 0.8 copy-done.5
  42.2 5.9 %collective-permute-done.2.refs_1_ = bf16[48,4224]{1,0:T(8,128)(2,1)} collective-permute-done((bf16[48,4224]{1,0:T(8,128)(2,1)S(1)}, bf16[48,4224]{1,0:T(8,128)(2,1)}, u32[]{:S(2)}, u32[]{:S(2)}) %collective-permute-start.2) | collective-permute-done | bytes 405536 | tf_op jit(solution)/shard_map/ppermute | solution.py:169
  48.1 3.0 %collective-permute-start.4 = (bf16[384,1920]{1,0:T(8,128)(2,1)S(1)}, bf16[384,1920]{1,0:T(8,128)(2,1)}, u32[]{:S(2)}, u32[]{:S(2)}) collective-permute-start(bf16[384,1920]{1,0:T(8,128)(2,1)S(1)} %bitcast.38), channel_id=1, source_target_pairs={{0,8},{8,0},{16,24},{24,16},{32,40},{40,32},{48,56},{56,48},{64,72... | collective-permute-start | bytes 4423688 | tf_op jit(solution)/shard_map/ppermute | solution.py:28
  51.1 0.6 fusion.18
  51.7 2.0 %fusion.16 = s32[384]{0:T(512)S(1)} fusion(s32[1,1,3,128]{3,2,1,0:T(4,128)S(1)} %get-tuple-element.62, s32[1,1,3,128]{3,2,1,0:T(4,128)S(1)} %get-tuple-element.61, s32[]{:T(128)} %bitcast.7, s32[]{:T(128)} %bitcast.9, s32[]{:T(128)} %bitcast.8), kind=kLoop, calls=%fused_computation.33 | loop fusion | flops 2304 | bytes 4620 | tf_op jit(solution)/shard_map/jit(_take)/gather | solution.py:360
  53.8 3.5 %collective-permute-start.8 = (bf16[48,4224]{1,0:T(8,128)(2,1)}, bf16[48,4224]{1,0:T(8,128)(2,1)}, u32[]{:S(2)}, u32[]{:S(2)}) collective-permute-start(bf16[48,4224]{1,0:T(8,128)(2,1)} %collective-permute-done.3.refs_5_), channel_id=1, source_target_pairs={{0,7},{1,0},{2,1},{3,2},{4,3},{5,4},{6,5},{7,6},{8,15},{9,8},{10,9... | collective-permute-start | bytes 1216520 | tf_op jit(solution)/shard_map/ppermute | solution.py:169
  57.3 3.1 %shard_map.104.packed_ref = bf16[384,1792]{1,0:T(8,128)(2,1)S(1)} custom-call(s32[1]{0:T(128)} %bitcast.core_ref, bf16[384,1920]{1,0:T(8,128)(2,1)S(1)} %bitcast.39, bf16[384,1920]{1,0:T(8,128)(2,1)} %collective-permute-done.4.other_ref), custom_call_target="tpu_custom_call" | custom-call | tf_op jit(solution)/shard_map/pallas_call | solution.py:109
  60.5 2.2 %fusion.1 = f32[16,384]{1,0:T(8,128)S(1)} fusion(bf16[384,1792]{1,0:T(8,128)(2,1)S(1)} %shard_map.104.packed_ref, bf16[1792,128]{1,0:T(8,128)(2,1)} %first_ref.1, s32[128]{0:T(128)S(1)} %and_select_fusion.1, s32[384]{0:T(512)S(1)} %and_select_fusion.2, s32[128]{0:T(128)S(1)} %and_select_fusion), kind=kOutput, calls=%fused_computation.4 | convolution fusion | flops 177883136 | bytes 1862144 | tf_op jit(solution)/shard_map/dot_general | solution.py:32
  62.7 3.2 %collective-permute-done.5 = f32[16,384]{1,0:T(8,128)S(1)} collective-permute-done((f32[16,384]{1,0:T(8,128)S(1)}, f32[16,384]{1,0:T(8,128)S(1)}, u32[]{:S(2)}, u32[]{:S(2)}) %collective-permute-start.5) | collective-permute-done | bytes 24608 | tf_op jit(solution)/shard_map/ppermute | solution.py:211
  65.8 2.5 %collective-permute-start.6 = (f32[16,384]{1,0:T(8,128)S(1)}, f32[16,384]{1,0:T(8,128)S(1)}, u32[]{:S(2)}, u32[]{:S(2)}) collective-permute-start(f32[16,384]{1,0:T(8,128)S(1)} %add.113), channel_id=1, source_target_pairs={{0,2},{1,3},{2,0},{3,1},{4,6},{5,7},{6,4},{7,5},{8,10},{9,11},{10,... | collective-permute-start | bytes 73736 | tf_op jit(solution)/shard_map/ppermute | solution.py:211
  68.3 0.9 slice.27
  69.3 1.0 slice.28
  70.3 4.0 %collective-permute-start.9 = (f32[16,384]{1,0:T(8,128)S(1)}, f32[16,384]{1,0:T(8,128)S(1)}, u32[]{:S(2)}, u32[]{:S(2)}) collective-permute-start(f32[16,384]{1,0:T(8,128)S(1)} %add.114), channel_id=1, source_target_pairs={{0,4},{1,5},{2,6},{3,7},{4,0},{5,1},{6,2},{7,3},{8,12},{9,13},{10,... | collective-permute-start | bytes 73736 | tf_op jit(solution)/shard_map/ppermute | solution.py:211
  74.4 2.5 %collective-permute-start.11 = (bf16[48,2176]{1,0:T(8,128)(2,1)S(1)}, bf16[48,2176]{1,0:T(8,128)(2,1)S(1)}, u32[]{:S(2)}, u32[]{:S(2)}) collective-permute-start(bf16[48,2176]{1,0:T(8,128)(2,1)S(1)} %slice.28), channel_id=1, source_target_pairs={{0,7},{1,0},{2,1},{3,2},{4,3},{5,4},{6,5},{7,6},{8,15},{9,8},{10,9... | collective-permute-start | bytes 626696 | tf_op jit(solution)/shard_map/ppermute | solution.py:169
  77.0 0.7 compare_select_fusion.inner_ref
  77.8 3.5 %collective-permute-done.10.refs_7_ = bf16[48,2048]{1,0:T(8,128)(2,1)S(1)} collective-permute-done((bf16[48,2048]{1,0:T(8,128)(2,1)S(1)}, bf16[48,2048]{1,0:T(8,128)(2,1)S(1)}, u32[]{:S(2)}, u32[]{:S(2)}) %collective-permute-start.10) | collective-permute-done | bytes 196640 | tf_op jit(solution)/shard_map/ppermute | solution.py:169
  81.3 1.8 %shard_map.105 = (bf16[8,48,4096]{2,1,0:T(8,128)(2,1)S(1)}, bf16[8,48,128]{2,1,0:T(8,128)(2,1)S(1)}) custom-call(s32[1]{0:T(128)} %bitcast.3.z_ref._, bf16[48,4224]{1,0:T(8,128)(2,1)} %collective-permute-done.7.refs_0_, bf16[48,4224]{1,0:T(8,128)(2,1)} %collective-permute-done.2.refs_1_, bf16[48,4224]{1,0:T(8,128)(2,1)S(1)} %copy-done.8, ...), custom_call_target="tpu_custom_call" | custom-call | tf_op jit(solution)/shard_map/pallas_call | solution.py:192
  83.1 1.6 %copy-done.3 = bf16[8,48,4096]{2,1,0:T(8,128)(2,1)} copy-done((bf16[8,48,4096]{2,1,0:T(8,128)(2,1)}, bf16[8,48,4096]{2,1,0:T(8,128)(2,1)S(1)}, u32[]{:S(2)}) %copy-start.3) | copy-done | bytes 3145752
  84.7 1.4 convolution_convert_fusion.first_ref
  86.1 2.4 %shard_map.106 = bf16[32,72,128]{2,1,0:T(8,128)(2,1)} custom-call(s32[1]{0:T(128)} %bitcast.3.z_ref._, bf16[128,384]{1,0:T(8,128)(2,1)} %compare_select_fusion.inner_ref, bf16[384,4096]{1,0:T(8,128)(2,1)} %bitcast.40, bf16[1792,128]{1,0:T(8,128)(2,1)} %convolution_convert_fusion.first_ref), custom_call_target="tpu_custom_call" | custom-call | tf_op jit(solution)/shard_map/pallas_call | solution.py:241
  88.5 8.2 %all-to-all-start.1 = ((bf16[32,72,128]{2,1,0:T(8,128)(2,1)}), bf16[32,72,128]{2,1,0:T(8,128)(2,1)S(1)}, u32[]{:S(2)}, u32[]{:S(2)}) async-start(bf16[32,72,128]{2,1,0:T(8,128)(2,1)} %shard_map.106), calls=%async_computation.1 | async-start | bytes 1179648 | tf_op jit(solution)/shard_map/all_to_all | solution.py:384
  96.8 10.7 %shard_map.107 = bf16[384,4096]{1,0:T(8,128)(2,1)} custom-call(bf16[384,1792]{1,0:T(8,128)(2,1)} %copy-done, bf16[4096,1792]{1,0:T(8,128)(2,1)} %all-gather.2.cloned.1.call-done.weight_ref), custom_call_target="tpu_custom_call" | custom-call | flops 5637144576 | bytes 19202048 | tf_op jit(solution)/shard_map/pallas_call | solution.py:297
  107.5 1.5 all-to-all-done.1
  109.1 1.4 collective-permute-start.12
  110.5 1.2 collective-permute-done.12
  111.7 0.9 collective-permute-start.13
  112.5 2.5 %collective-permute-done.13 = bf16[32,128]{1,0:T(8,128)(2,1)S(1)} collective-permute-done((bf16[32,128]{1,0:T(8,128)(2,1)S(1)}, bf16[32,128]{1,0:T(8,128)(2,1)S(1)}, u32[]{:S(2)}, u32[]{:S(2)}) %collective-permute-start.13) | collective-permute-done | bytes 8224 | tf_op jit(solution)/shard_map/ppermute | solution.py:219
  115.1 2.8 %collective-permute-start.14 = (bf16[64,128]{1,0:T(8,128)(2,1)S(1)}, bf16[64,128]{1,0:T(8,128)(2,1)S(1)}, u32[]{:S(2)}, u32[]{:S(2)}) collective-permute-start(bf16[64,128]{1,0:T(8,128)(2,1)S(1)} %pad_maximum_fusion.1), channel_id=1, source_target_pairs={{0,4},{1,5},{2,6},{3,7},{4,0},{5,1},{6,2},{7,3},{8,12},{9,13},{10,... | collective-permute-start | bytes 49160 | tf_op jit(solution)/shard_map/ppermute | solution.py:219
  117.9 3.8 %collective-permute-done.14 = bf16[64,128]{1,0:T(8,128)(2,1)S(1)} collective-permute-done((bf16[64,128]{1,0:T(8,128)(2,1)S(1)}, bf16[64,128]{1,0:T(8,128)(2,1)S(1)}, u32[]{:S(2)}, u32[]{:S(2)}) %collective-permute-start.14) | collective-permute-done | bytes 16416 | tf_op jit(solution)/shard_map/ppermute | solution.py:219
  121.7 1.0 broadcast_in_dim.39
  122.6 5.1 %all-to-all-start.2 = ((bf16[16,184,128]{2,1,0:T(8,128)(2,1)}), bf16[16,184,128]{2,1,0:T(8,128)(2,1)S(1)}, u32[]{:S(2)}, u32[]{:S(2)}) async-start(bf16[16,184,128]{2,1,0:T(8,128)(2,1)} %broadcast_in_dim.39), calls=%async_computation.3 | async-start | bytes 1507328 | tf_op jit(solution)/shard_map/all_to_all | solution.py:389
  127.8 12.4 %shard_map.108 = bf16[384,1792]{1,0:T(8,128)(2,1)} custom-call(bf16[384,4096]{1,0:T(8,128)(2,1)} %bitcast.41, bf16[384,128]{1,0:T(8,128)(2,1)} %bitcast.43, bf16[4096,1792]{1,0:T(8,128)(2,1)} %all-gather.2.cloned.1.call-done.weight_ref, bf16[1792,128]{1,0:T(8,128)(2,1)} %first_ref.1), custom_call_target="tpu_custom_call" | custom-call | flops 5637144576 | bytes 19202048 | tf_op jit(solution)/shard_map/pallas_call | solution.py:323
  140.2 4.2 %collective-permute-start.15 = (bf16[16,184,128]{2,1,0:T(8,128)(2,1)S(1)}, bf16[16,184,128]{2,1,0:T(8,128)(2,1)S(1)}, u32[]{:S(2)}, u32[]{:S(2)}) collective-permute-start(bf16[16,184,128]{2,1,0:T(8,128)(2,1)S(1)} %all-to-all-done.2.mine_ref), channel_id=1, source_target_pairs={{0,8},{8,0},{16,24},{24,16},{32,40},{40,32},{48,56},{56,48},{64,72... | collective-permute-start | bytes 2261000 | tf_op jit(solution)/shard_map/ppermute | solution.py:28
  144.5 0.5 convolution_multiply_fusion
  145.0 1.3 collective-permute-done.15.other_ref
  146.2 2.5 %shard_map.109 = (f32[1792,128]{1,0:T(8,128)}, f32[128,4096]{1,0:T(8,128)}) custom-call(s32[2]{0:T(128)S(1)} %pad_add_fusion.place_ref, bf16[16,184,128]{2,1,0:T(8,128)(2,1)S(1)} %all-to-all-done.2.mine_ref, bf16[16,184,128]{2,1,0:T(8,128)(2,1)S(1)} %collective-permute-done.15.other_ref), custom_call_target="tpu_custom_call" | custom-call | tf_op jit(solution)/shard_map/pallas_call | solution.py:278
  148.8 1.7 %reduce-scatter.2.cloned.1.call-done = bf16[48,4096]{1,0:T(8,128)(2,1)} async-done(((bf16[384,4096]{1,0:T(8,128)(2,1)}), bf16[48,4096]{1,0:T(8,128)(2,1)}) %reduce-scatter.2.cloned.1.call-update) | async-done | bytes 393232 | tf_op jit(solution)/shard_map/reduce_scatter | solution.py:395
  150.5 1.8 %add_convert_fusion = bf16[48,4096]{1,0:T(8,128)(2,1)} fusion(f32[48,4096]{1,0:T(8,128)S(1)} %convolution_multiply_fusion, bf16[48,4096]{1,0:T(8,128)(2,1)} %reduce-scatter.2.cloned.1.call-done), kind=kLoop, calls=%fused_computation.6 | loop fusion | flops 589824 | bytes 1572864 | tf_op jit(solution)/shard_map/convert_element_type | solution.py:400
  (58 shorter events, 0.8 us)
Async XLA Ops:
  7.2 2.2 %copy-start.13 = (s32[384]{0:T(512)S(1)}, s32[384]{0:T(512)}, u32[]{:S(2)}) copy-start(s32[384]{0:T(512)} %param.10) | copy-start | bytes 4612
  7.2 2.2 %copy-start.4 = (bf16[384,1792]{1,0:T(8,128)(2,1)S(1)}, bf16[384,1792]{1,0:T(8,128)(2,1)}, u32[]{:S(2)}) copy-start(bf16[384,1792]{1,0:T(8,128)(2,1)} %hidden_ref.1) | copy-start | bytes 4128772
  7.2 89.6 %all-gather.2.cloned.1.call-start = ((), (), s32[]{:S(2)}) async-start(), calls=%async_computation.4 | async-start | bytes 15138816 | tf_op jit(solution)/shard_map/all_gather | solution.py:350
  11.6 7.7 %copy-start.1 = (bf16[128,4096]{1,0:T(8,128)(2,1)S(1)}, bf16[128,4096]{1,0:T(8,128)(2,1)}, u32[]{:S(2)}) copy-start(bf16[128,4096]{1,0:T(8,128)(2,1)} %second_ref.1) | copy-start | bytes 3145732
  11.6 7.7 %copy-start.11 = (s32[3]{0:T(128)S(1)}, s32[3]{0:T(128)}, u32[]{:S(2)}) copy-start(s32[3]{0:T(128)} %jobs_ref.1) | copy-start | bytes 40
  11.6 36.5 %all-to-all-start = ((bf16[16,24,1920]{2,1,0:T(8,128)(2,1)}), bf16[16,24,1920]{2,1,0:T(8,128)(2,1)S(1)}, u32[]{:S(2)}, u32[]{:S(2)}) async-start(bf16[16,24,1920]{2,1,0:T(8,128)(2,1)} %bitcast.1), calls=%async_computation | async-start | bytes 2949120 | tf_op jit(solution)/shard_map/all_to_all | solution.py:352
  19.4 1.0 copy-start.9
  21.4 13.4 %collective-permute-start.1 = (bf16[48,4224]{1,0:T(8,128)(2,1)S(1)}, bf16[48,4224]{1,0:T(8,128)(2,1)S(1)}, u32[]{:S(2)}, u32[]{:S(2)}) collective-permute-start(bf16[48,4224]{1,0:T(8,128)(2,1)S(1)} %shard_map.103.refs_3_), channel_id=1, source_target_pairs={{0,7},{1,0},{2,1},{3,2},{4,3},{5,4},{6,5},{7,6},{8,15},{9,8},{10,9... | collective-permute-start | bytes 1216520 | tf_op jit(solution)/shard_map/ppermute | solution.py:169
  27.0 10.9 %collective-permute-start = (bf16[48,4224]{1,0:T(8,128)(2,1)S(1)}, bf16[48,4224]{1,0:T(8,128)(2,1)S(1)}, u32[]{:S(2)}, u32[]{:S(2)}) collective-permute-start(bf16[48,4224]{1,0:T(8,128)(2,1)S(1)} %shard_map.103.refs_3_), channel_id=1, source_target_pairs={{0,1},{1,2},{2,3},{3,4},{4,5},{5,6},{6,7},{7,0},{8,9},{9,10},{10,1... | collective-permute-start | bytes 1216520 | tf_op jit(solution)/shard_map/ppermute | solution.py:169
  38.0 10.1 %collective-permute-start.2 = (bf16[48,4224]{1,0:T(8,128)(2,1)S(1)}, bf16[48,4224]{1,0:T(8,128)(2,1)}, u32[]{:S(2)}, u32[]{:S(2)}) collective-permute-start(bf16[48,4224]{1,0:T(8,128)(2,1)S(1)} %collective-permute-done.refs_2_), channel_id=1, source_target_pairs={{0,1},{1,2},{2,3},{3,4},{4,5},{5,6},{6,7},{7,0},{8,9},{9,10},{10,1... | collective-permute-start | bytes 1216520 | tf_op jit(solution)/shard_map/ppermute | solution.py:169
  38.0 0.8 copy-start.7
  38.8 9.4 %collective-permute-start.3 = (bf16[48,4224]{1,0:T(8,128)(2,1)S(1)}, bf16[48,4224]{1,0:T(8,128)(2,1)}, u32[]{:S(2)}, u32[]{:S(2)}) collective-permute-start(bf16[48,4224]{1,0:T(8,128)(2,1)S(1)} %collective-permute-done.1.refs_4_), channel_id=1, source_target_pairs={{0,7},{1,0},{2,1},{3,2},{4,3},{5,4},{6,5},{7,6},{8,15},{9,8},{10,9... | collective-permute-start | bytes 1216520 | tf_op jit(solution)/shard_map/ppermute | solution.py:169
  41.4 0.8 copy-start.5
  48.1 9.1 %collective-permute-start.4 = (bf16[384,1920]{1,0:T(8,128)(2,1)S(1)}, bf16[384,1920]{1,0:T(8,128)(2,1)}, u32[]{:S(2)}, u32[]{:S(2)}) collective-permute-start(bf16[384,1920]{1,0:T(8,128)(2,1)S(1)} %bitcast.38), channel_id=1, source_target_pairs={{0,8},{8,0},{16,24},{24,16},{32,40},{40,32},{48,56},{56,48},{64,72... | collective-permute-start | bytes 4423688 | tf_op jit(solution)/shard_map/ppermute | solution.py:28
  53.7 14.6 %collective-permute-start.7 = (bf16[48,4224]{1,0:T(8,128)(2,1)}, bf16[48,4224]{1,0:T(8,128)(2,1)}, u32[]{:S(2)}, u32[]{:S(2)}) collective-permute-start(bf16[48,4224]{1,0:T(8,128)(2,1)} %collective-permute-done.2.refs_1_), channel_id=1, source_target_pairs={{0,1},{1,2},{2,3},{3,4},{4,5},{5,6},{6,7},{7,0},{8,9},{9,10},{10,1... | collective-permute-start | bytes 1216520 | tf_op jit(solution)/shard_map/ppermute | solution.py:169
  53.8 14.5 %collective-permute-start.8 = (bf16[48,4224]{1,0:T(8,128)(2,1)}, bf16[48,4224]{1,0:T(8,128)(2,1)}, u32[]{:S(2)}, u32[]{:S(2)}) collective-permute-start(bf16[48,4224]{1,0:T(8,128)(2,1)} %collective-permute-done.3.refs_5_), channel_id=1, source_target_pairs={{0,7},{1,0},{2,1},{3,2},{4,3},{5,4},{6,5},{7,6},{8,15},{9,8},{10,9... | collective-permute-start | bytes 1216520 | tf_op jit(solution)/shard_map/ppermute | solution.py:169
  60.4 24.3 %copy-start = (bf16[384,1792]{1,0:T(8,128)(2,1)}, bf16[384,1792]{1,0:T(8,128)(2,1)S(1)}, u32[]{:S(2)}) copy-start(bf16[384,1792]{1,0:T(8,128)(2,1)S(1)} %shard_map.104.packed_ref) | copy-start | bytes 4128772
  60.4 20.8 %copy-start.6 = (bf16[48,4224]{1,0:T(8,128)(2,1)S(1)}, bf16[48,4224]{1,0:T(8,128)(2,1)}, u32[]{:S(2)}) copy-start(bf16[48,4224]{1,0:T(8,128)(2,1)} %copy-done.5) | copy-start | bytes 1216516
  60.4 20.8 %copy-start.8 = (bf16[48,4224]{1,0:T(8,128)(2,1)S(1)}, bf16[48,4224]{1,0:T(8,128)(2,1)}, u32[]{:S(2)}) copy-start(bf16[48,4224]{1,0:T(8,128)(2,1)} %copy-done.7) | copy-start | bytes 1216516
  62.7 3.2 %collective-permute-start.5 = (f32[16,384]{1,0:T(8,128)S(1)}, f32[16,384]{1,0:T(8,128)S(1)}, u32[]{:S(2)}, u32[]{:S(2)}) collective-permute-start(f32[16,384]{1,0:T(8,128)S(1)} %fusion.1), channel_id=1, source_target_pairs={{0,1},{1,0},{2,3},{3,2},{4,5},{5,4},{6,7},{7,6},{8,9},{9,8},{10,11... | collective-permute-start | bytes 73736 | tf_op jit(solution)/shard_map/ppermute | solution.py:211
  65.8 4.4 %collective-permute-start.6 = (f32[16,384]{1,0:T(8,128)S(1)}, f32[16,384]{1,0:T(8,128)S(1)}, u32[]{:S(2)}, u32[]{:S(2)}) collective-permute-start(f32[16,384]{1,0:T(8,128)S(1)} %add.113), channel_id=1, source_target_pairs={{0,2},{1,3},{2,0},{3,1},{4,6},{5,7},{6,4},{7,5},{8,10},{9,11},{10,... | collective-permute-start | bytes 73736 | tf_op jit(solution)/shard_map/ppermute | solution.py:211
  70.3 6.8 %collective-permute-start.9 = (f32[16,384]{1,0:T(8,128)S(1)}, f32[16,384]{1,0:T(8,128)S(1)}, u32[]{:S(2)}, u32[]{:S(2)}) collective-permute-start(f32[16,384]{1,0:T(8,128)S(1)} %add.114), channel_id=1, source_target_pairs={{0,4},{1,5},{2,6},{3,7},{4,0},{5,1},{6,2},{7,3},{8,12},{9,13},{10,... | collective-permute-start | bytes 73736 | tf_op jit(solution)/shard_map/ppermute | solution.py:211
  74.3 7.0 %collective-permute-start.10 = (bf16[48,2048]{1,0:T(8,128)(2,1)S(1)}, bf16[48,2048]{1,0:T(8,128)(2,1)S(1)}, u32[]{:S(2)}, u32[]{:S(2)}) collective-permute-start(bf16[48,2048]{1,0:T(8,128)(2,1)S(1)} %slice.27), channel_id=1, source_target_pairs={{0,1},{1,2},{2,3},{3,4},{4,5},{5,6},{6,7},{7,0},{8,9},{9,10},{10,1... | collective-permute-start | bytes 589832 | tf_op jit(solution)/shard_map/ppermute | solution.py:169
  74.4 6.8 %collective-permute-start.11 = (bf16[48,2176]{1,0:T(8,128)(2,1)S(1)}, bf16[48,2176]{1,0:T(8,128)(2,1)S(1)}, u32[]{:S(2)}, u32[]{:S(2)}) collective-permute-start(bf16[48,2176]{1,0:T(8,128)(2,1)S(1)} %slice.28), channel_id=1, source_target_pairs={{0,7},{1,0},{2,1},{3,2},{4,3},{5,4},{6,5},{7,6},{8,15},{9,8},{10,9... | collective-permute-start | bytes 626696 | tf_op jit(solution)/shard_map/ppermute | solution.py:169
  83.1 1.6 %copy-start.3 = (bf16[8,48,4096]{2,1,0:T(8,128)(2,1)}, bf16[8,48,4096]{2,1,0:T(8,128)(2,1)S(1)}, u32[]{:S(2)}) copy-start(bf16[8,48,4096]{2,1,0:T(8,128)(2,1)S(1)} %get-tuple-element.51) | copy-start | bytes 9437188
  84.7 3.7 %copy-start.10 = (bf16[8,48,128]{2,1,0:T(8,128)(2,1)}, bf16[8,48,128]{2,1,0:T(8,128)(2,1)S(1)}, u32[]{:S(2)}) copy-start(bf16[8,48,128]{2,1,0:T(8,128)(2,1)S(1)} %get-tuple-element.52) | copy-start | bytes 294916
  88.5 20.5 %all-to-all-start.1 = ((bf16[32,72,128]{2,1,0:T(8,128)(2,1)}), bf16[32,72,128]{2,1,0:T(8,128)(2,1)S(1)}, u32[]{:S(2)}, u32[]{:S(2)}) async-start(bf16[32,72,128]{2,1,0:T(8,128)(2,1)} %shard_map.106), calls=%async_computation.1 | async-start | bytes 1179648 | tf_op jit(solution)/shard_map/all_to_all | solution.py:384
  96.7 53.8 %reduce-scatter.2.cloned.1.call-start = ((), (), s32[]{:S(2)}) async-start(), calls=%async_computation.5 | async-start | bytes 3538944 | tf_op jit(solution)/shard_map/reduce_scatter | solution.py:395
  109.1 2.5 %collective-permute-start.12 = (bf16[16,128]{1,0:T(8,128)(2,1)S(1)}, bf16[16,128]{1,0:T(8,128)(2,1)S(1)}, u32[]{:S(2)}, u32[]{:S(2)}) collective-permute-start(bf16[16,128]{1,0:T(8,128)(2,1)S(1)} %slice.34), channel_id=1, source_target_pairs={{0,1},{1,0},{2,3},{3,2},{4,5},{5,4},{6,7},{7,6},{8,9},{9,8},{10,11... | collective-permute-start | bytes 12296 | tf_op jit(solution)/shard_map/ppermute | solution.py:219
  111.7 3.4 %collective-permute-start.13 = (bf16[32,128]{1,0:T(8,128)(2,1)S(1)}, bf16[32,128]{1,0:T(8,128)(2,1)S(1)}, u32[]{:S(2)}, u32[]{:S(2)}) collective-permute-start(bf16[32,128]{1,0:T(8,128)(2,1)S(1)} %pad_maximum_fusion.2), channel_id=1, source_target_pairs={{0,2},{1,3},{2,0},{3,1},{4,6},{5,7},{6,4},{7,5},{8,10},{9,11},{10,... | collective-permute-start | bytes 24584 | tf_op jit(solution)/shard_map/ppermute | solution.py:219
  115.1 6.6 %collective-permute-start.14 = (bf16[64,128]{1,0:T(8,128)(2,1)S(1)}, bf16[64,128]{1,0:T(8,128)(2,1)S(1)}, u32[]{:S(2)}, u32[]{:S(2)}) collective-permute-start(bf16[64,128]{1,0:T(8,128)(2,1)S(1)} %pad_maximum_fusion.1), channel_id=1, source_target_pairs={{0,4},{1,5},{2,6},{3,7},{4,0},{5,1},{6,2},{7,3},{8,12},{9,13},{10,... | collective-permute-start | bytes 49160 | tf_op jit(solution)/shard_map/ppermute | solution.py:219
  122.6 17.6 %all-to-all-start.2 = ((bf16[16,184,128]{2,1,0:T(8,128)(2,1)}), bf16[16,184,128]{2,1,0:T(8,128)(2,1)S(1)}, u32[]{:S(2)}, u32[]{:S(2)}) async-start(bf16[16,184,128]{2,1,0:T(8,128)(2,1)} %broadcast_in_dim.39), calls=%async_computation.3 | async-start | bytes 1507328 | tf_op jit(solution)/shard_map/all_to_all | solution.py:389
  127.8 16.7 %copy-start.2 = (bf16[128,4096]{1,0:T(8,128)(2,1)S(1)}, bf16[128,4096]{1,0:T(8,128)(2,1)}, u32[]{:S(2)}) copy-start(bf16[128,4096]{1,0:T(8,128)(2,1)} %second_ref.1) | copy-start | bytes 3145732
  127.8 16.7 %copy-start.12 = (bf16[128,384]{1,0:T(8,128)(2,1)S(1)}, bf16[128,384]{1,0:T(8,128)(2,1)}, u32[]{:S(2)}) copy-start(bf16[128,384]{1,0:T(8,128)(2,1)} %compare_select_fusion.inner_ref) | copy-start | bytes 294916
  140.2 6.1 %collective-permute-start.15 = (bf16[16,184,128]{2,1,0:T(8,128)(2,1)S(1)}, bf16[16,184,128]{2,1,0:T(8,128)(2,1)S(1)}, u32[]{:S(2)}, u32[]{:S(2)}) collective-permute-start(bf16[16,184,128]{2,1,0:T(8,128)(2,1)S(1)} %all-to-all-done.2.mine_ref), channel_id=1, source_target_pairs={{0,8},{8,0},{16,24},{24,16},{32,40},{40,32},{48,56},{56,48},{64,72... | collective-permute-start | bytes 2261000 | tf_op jit(solution)/shard_map/ppermute | solution.py:28
Sparse Core Ops, SparseCore 0:
  10.6 85.0 all-gather.1
  109.1 41.3 reduce-scatter.1
